TPU v7x, 32 devices: a whole 2x2x4 slice. The times are simulated.
32 devices in a mesh: fsdp: 8 (over z, x), tp: 4 (over y, core).
Axes of the slice: x: 2, y: 2, z: 4, core: 2. Of those that a mesh axis runs over, the one named last changes fastest.
Arguments:
- tokens: bfloat16 [16384, 768], P(('fsdp', 'tp')), may hold values from -6 to 6
- segment_ids: int32 [16384], P('fsdp'), may hold values from 0 to 127, never falling along the last dimension, each value on 1 to 512 neighbouring positions
- query_weight: bfloat16 [768, 768], P('fsdp', 'tp'), may hold values from -0.21875 to 0.21875
- key_weight: bfloat16 [768, 768], P('fsdp', 'tp'), may hold values from -0.21875 to 0.21875
- value_weight: bfloat16 [768, 768], P('fsdp', 'tp'), may hold values from -0.21875 to 0.21875
- query_bias: float32 [768], replicated, may hold values from -3 to 3
- value_bias: float32 [768], replicated, may hold values from -3 to 3
- output_weight: bfloat16 [768, 768], P('tp', 'fsdp'), may hold values from -0.625 to 0.625
- output_bias: float32 [768], replicated, may hold values from -3 to 3
- first_gain: float32 [768], replicated, may hold values from 0.1 to 1.9
- first_shift: float32 [768], replicated, may hold values from -3 to 3
- up_weight: bfloat16 [768, 3072], P('fsdp', 'tp'), may hold values from -0.21875 to 0.21875
- up_bias: float32 [3072], replicated, may hold values from -3 to 3
- down_weight: bfloat16 [3072, 768], P('tp', 'fsdp'), may hold values from -0.109375 to 0.109375
- down_bias: float32 [768], replicated, may hold values from -3 to 3
- second_gain: float32 [768], replicated, may hold values from 0.1 to 1.9
- second_shift: float32 [768], replicated, may hold values from -3 to 3
- cotangent: bfloat16 [16384, 768], P(('fsdp', 'tp')), may hold values from -6 to 6
Outputs:
- layer_output: float32 [16384, 768], P(('fsdp', 'tp'))
- input_grad: float32 [16384, 768], P(('fsdp', 'tp'))
- query_weight_grad: float32 [768, 768], P('fsdp', 'tp')
- key_weight_grad: float32 [768, 768], P('fsdp', 'tp')
- value_weight_grad: float32 [768, 768], P('fsdp', 'tp')
- query_bias_grad: float32 [768], P('tp')
- value_bias_grad: float32 [768], P('tp')
- output_weight_grad: float32 [768, 768], P('tp', 'fsdp')
- output_bias_grad: float32 [768], replicated
- first_gain_grad: float32 [768], replicated
- first_shift_grad: float32 [768], replicated
- up_weight_grad: float32 [768, 3072], P('fsdp', 'tp')
- up_bias_grad: float32 [3072], P('tp')
- down_weight_grad: float32 [3072, 768], P('tp', 'fsdp')
- down_bias_grad: float32 [768], replicated
- second_gain_grad: float32 [768], replicated
- second_shift_grad: float32 [768], replicated
Inputs may be any that keep to these rules, and one draw needn't show every extreme that they name: segment_ids never fall along the tokens; each document holds 1 to 512 tokens, and one holds exactly 512.
All inputs are finite; a program needn't handle non-finite values.
Results may differ from a plain program's by a relative error of at most 0.018.
Values may be sent and summed in bfloat16 or wider, within the bound.
No kernel may reach another device: no remote copies, remote signals or barrier semaphores. Data moves between devices by JAX's collectives and lax.ppermute only.
A program may use at most 128 MiB of HBM per device.

v0:
```python
from functools import partial
import math

import jax
import jax.numpy as jnp
import numpy as np
from jax import lax
from jax.experimental import pallas as pl
from jax.experimental.pallas import tpu as pltpu
from jax.sharding import PartitionSpec as P

HD = 64
SEQ = 512
AXES = ("fsdp", "tp")
F32 = jnp.float32
BF16 = jnp.bfloat16
CUTS = 8
MIB = 1 << 20


def exchange_plan(fsdp, tp):
    count = fsdp * tp
    if (fsdp, tp) == (8, 4):
        select, pairs = 1, [(8, 16), (4, 2), (16, 8), (2, 4)]
    else:
        select = tp
        pairs = [(1 << i,) * 2 for i in range(count.bit_length() - 1) if 1 << i != select]
    steps = [[d ^ pair[1 if d & select else 0] for d in range(count)] for pair in pairs]
    steps.append([d ^ select for d in range(count)])
    sources = [[d] for d in range(count)]
    for step in steps:
        sources = [sources[d] + sources[step[d]] for d in range(count)]
    return steps, np.array(sources)


def swap(array, step):
    return lax.ppermute(array, AXES, list(enumerate(step)))


def after(array, *others):
    return lax.optimization_barrier((array, *others))[0]


class Gather:
    def __init__(self, shard, steps):
        self.steps, self.at, self.held, self.pieces = steps, 0, shard[None], None

    def step(self, *others):
        step = self.steps[self.at]
        self.at += 1
        if others:
            self.held = after(self.held, *others)
        moved = swap(self.held, step)
        if self.at == len(self.steps) - 1:
            self.pieces = [self.held, moved]
        else:
            self.held = jnp.concatenate([self.held, moved], axis=0)
        return moved

    def split(self):
        parts = []
        for i in range(self.held.shape[1]):
            part = Gather(self.held[0, i], self.steps)
            part.at, part.held = self.at, self.held[:, i]
            parts.append(part)
        return parts

    def finish(self, *others):
        pieces = [after(piece, *others) for piece in self.pieces] if others else self.pieces
        return self.pieces + [swap(piece, self.steps[-1]) for piece in pieces]


class Sum:
    def __init__(self, keep, send, steps, extra=0):
        self.steps, self.at, self.keep, self.send, self.extra = steps, len(steps) - 1, keep, send, extra

    def add(self, keep, moved):
        keep, moved = keep.astype(F32), moved.astype(F32)
        if not self.extra:
            return keep + moved
        rows = keep.shape[1] - 2 * self.extra
        total = (keep + moved)[:, :rows]
        high = slice(rows, rows + self.extra)
        low = slice(rows + self.extra, None)
        side = (keep[:, high] + keep[:, low]) + (moved[:, high] + moved[:, low])
        if self.at == 0:
            return total, side
        high = lax.reduce_precision(side, 8, 7)
        return jnp.concatenate([total, high, side - high], axis=1)

    def start(self, *others):
        send = after(self.send, *others) if others else self.send
        half = send.shape[0] // 2
        parts = [send[:half], send[half:]] if self.at == len(self.steps) - 1 else [send]
        self.moved = [swap(part, self.steps[self.at]) for part in parts]

    def hold(self, *others):
        self.moved = list(lax.optimization_barrier((*self.moved, *others))[: len(self.moved)])

    def end(self):
        if self.at == 0:
            return self.add(self.keep, self.moved[0])
        half = self.keep.shape[0] // 2
        if len(self.moved) == 1:
            moved = self.moved[0][:half], self.moved[0][half:]
        else:
            moved = self.moved
        send = self.add(self.keep[half:], moved[1]).astype(BF16)
        keep = self.add(self.keep[:half], moved[0]).astype(BF16)
        self.keep, self.send = keep, send
        self.at -= 1
        return send

    def step(self, *others):
        self.start(*others)
        return self.end()

    @staticmethod
    def merge(*packages):
        one = packages[0]
        keep, send = (
            jnp.stack([getattr(package, name) for package in packages], axis=1) for name in ("keep", "send")
        )
        merged = Sum(keep, send, one.steps)
        merged.at = one.at
        return merged


def both(*packages):
    moved = lax.optimization_barrier([package.moved for package in packages])
    for package, arrived in zip(packages, moved):
        package.moved = arrived
        package.end()


def copy_block(order_ref, from_ref, to_ref):
    to_ref[...] = from_ref[...]


def laid_out(blocks, slot_of, fsdp, tp):
    _, rows, cols = blocks.shape
    grid_spec = pltpu.PrefetchScalarGridSpec(
        num_scalar_prefetch=1,
        grid=(fsdp, tp),
        in_specs=[pl.BlockSpec((1, rows, cols), lambda f, t, s: (s[f * tp + t], 0, 0))],
        out_specs=pl.BlockSpec((1, rows, cols), lambda f, t, s: (f, 0, t)),
    )
    return pl.pallas_call(
        copy_block,
        grid_spec=grid_spec,
        out_shape=jax.ShapeDtypeStruct((fsdp, rows, tp * cols), blocks.dtype),
    )(slot_of, blocks)


def cut_up(full, slot_of, fsdp, tp):
    _, rows, cols = full.shape
    cols = cols // tp
    grid_spec = pltpu.PrefetchScalarGridSpec(
        num_scalar_prefetch=1,
        grid=(fsdp, tp),
        in_specs=[pl.BlockSpec((1, rows, cols), lambda f, t, s: (f, 0, t))],
        out_specs=pl.BlockSpec((1, rows, cols), lambda f, t, s: (s[f * tp + t], 0, 0)),
    )
    return pl.pallas_call(
        copy_block,
        grid_spec=grid_spec,
        out_shape=jax.ShapeDtypeStruct((fsdp * tp, rows, cols), full.dtype),
    )(slot_of, full)


def dot(a, b):
    return lax.dot_general(a, b, (((1,), (0,)), ((), ())), preferred_element_type=F32)


def dot_nt(a, b):
    return lax.dot_general(a, b, (((1,), (1,)), ((), ())), preferred_element_type=F32)


def dot_tn(a, b):
    return lax.dot_general(a, b, (((0,), (0,)), ((), ())), preferred_element_type=F32)


def norm_forward(values):
    average = jnp.mean(values, axis=-1, keepdims=True)
    centered = values - average
    inverse = lax.rsqrt(jnp.mean(centered * centered, axis=-1, keepdims=True) + 1e-12)
    return centered * inverse, inverse


def norm_backward(upstream, normal, inverse, gain):
    scaled = upstream * gain
    return inverse * (
        scaled
        - jnp.mean(scaled, axis=-1, keepdims=True)
        - normal * jnp.mean(scaled * normal, axis=-1, keepdims=True)
    )


def gelu_parts(x):
    below = 0.5 + 0.5 * lax.erf(x * math.sqrt(0.5))
    return x * below, below + x * (jnp.exp(-0.5 * (x * x)) * (1.0 / math.sqrt(2.0 * math.pi)))


def column_sum(array):
    return jnp.sum(array, axis=0, keepdims=True)


def each(count, step):
    lax.fori_loop(0, count, lambda i, carry: (step(i), carry)[1], 0)


def assemble(half, place_ref, pieces, weight):
    rows = weight.shape[1] // CUTS
    per = pieces[0].shape[0]
    for at, piece in enumerate(pieces):

        def copy(slot, at=at, piece=piece):
            place = place_ref[(half * len(pieces) + at) * per + slot]
            i = place // CUTS
            cut = place - i * CUTS
            weight[i, pl.ds(pl.multiple_of(cut * rows, rows), rows), :] = piece[slot]

        each(per, copy)


def put_blocks(half, slot_ref, out_ref, i, value, cols=slice(None)):
    rows = value.shape[0] // CUTS
    for cut in range(CUTS):
        slot = slot_ref[half * out_ref.shape[0] + i * CUTS + cut]
        out_ref[slot, :rows, cols] = value[cut * rows : (cut + 1) * rows].astype(out_ref.dtype)


def attention_kernel(half, place_ref, turn_ref, tokens_ref, ids_row, ids_col, bias_ref, *rest):
    if half == 0:
        output_bias, *rest = rest
        *pieces, weight, qkv_ref, context_ref, exponent_ref, total_ref, acc, turned_ref, mask = rest
        acc[...] = tokens_ref[...].astype(F32) + output_bias[...]
        turned_ref[...] = tokens_ref[...].T
    else:
        acc_ref, gain, shift, *rest = rest
        *pieces, weight, qkv_ref, context_ref, exponent_ref, total_ref = rest[:-5]
        normal_ref, inverse_ref, low_ref, mask, acc = rest[-5:]
        acc[...] = acc_ref[...]
    cols = context_ref.shape[1]
    count = weight.shape[0]
    assemble(half, place_ref, pieces, weight)
    mask[...] = jnp.where(ids_col[...] == ids_row[...], 0.0, -1e30)

    def step(i):
        bias = bias_ref[turn_ref[half * count + i]]
        qkv = (dot(tokens_ref[...], weight[i, :, : 3 * cols]) + bias).astype(BF16)
        qkv_ref[i] = qkv
        contexts = []
        for h in range(cols // HD):
            queries, keys, values = (
                qkv[:, part * cols + h * HD : part * cols + (h + 1) * HD] for part in range(3)
            )
            scores = dot_nt(keys, queries * (HD**-0.5)) + mask[...]
            top = jnp.max(scores, axis=0, keepdims=True)
            exponent = jnp.exp(scores - top)
            total = 1.0 / jnp.sum(exponent, axis=0, keepdims=True)
            exponent = exponent.astype(BF16)
            exponent_ref[i, h] = exponent
            contexts.append((dot_tn(values, exponent) * total).astype(BF16))
            total_ref[i, h : h + 1] = total
        context = jnp.concatenate(contexts, axis=0)
        context_ref[i] = context
        acc[...] += dot_nt(context.T, weight[i, :, 3 * cols :])

    each(count, step)
    if half == 1:
        normal, inverse = norm_forward(acc[...])
        normal_ref[...] = normal
        inverse_ref[...] = inverse
        low_ref[...] = (normal * gain[...] + shift[...]).astype(BF16)


def up_kernel(place_ref, turn_ref, low_ref, bias_ref, *rest):
    *pieces, weight_first, active_first, slope_first, weight_second, active_second, slope_second = rest
    many = len(pieces) // 2
    up_half(0, place_ref, turn_ref, low_ref, bias_ref, pieces[:many], weight_first, active_first, slope_first)
    up_half(1, place_ref, turn_ref, low_ref, bias_ref, pieces[many:], weight_second, active_second, slope_second)


def up_half(half, place_ref, turn_ref, low_ref, bias_ref, pieces, weight, active_ref, slope_ref):
    count = weight.shape[0]
    assemble(half, place_ref, pieces, weight)

    def step(i):
        pre = dot(low_ref[...], weight[i]) + bias_ref[turn_ref[half * count + i]]
        active, slope = gelu_parts(pre)
        active_ref[i] = active.astype(BF16)
        slope_ref[i] = slope.astype(BF16)

    each(count, step)


def down_first_kernel(place_ref, active_ref, normal_ref, first_gain, first_shift, bias_ref, *rest):
    *pieces, weight, acc = rest
    assemble(0, place_ref, pieces, weight)
    acc[...] = normal_ref[...] * first_gain[...] + (first_shift[...] + bias_ref[...])

    def step(i):
        acc[...] += dot_nt(active_ref[i], weight[i])

    each(weight.shape[0], step)


def down_second_kernel(place_ref, slot_ref, active_ref, acc_ref, gain, shift, cotangent_ref, *rest):
    *pieces, weight, output_ref, grad_ref, low_ref, turned_ref, sums_ref, send_ref, acc = rest
    count = weight.shape[0]
    assemble(1, place_ref, pieces, weight)
    acc[...] = acc_ref[...]

    def step(i):
        acc[...] += dot_nt(active_ref[i], weight[i])

    each(count, step)
    normal, inverse = norm_forward(acc[...])
    output_ref[...] = normal * gain[...] + shift[...]
    upstream = cotangent_ref[...].astype(F32)
    grad = norm_backward(upstream, normal, inverse, gain[...])
    grad_ref[...] = grad
    low = grad.astype(BF16)
    low_ref[...] = low
    turned_ref[...] = low.T
    sums_ref[0:1] = column_sum(grad)
    sums_ref[1:2] = column_sum(upstream * normal)
    sums_ref[2:3] = column_sum(upstream)
    each(count, lambda i: put_blocks(1, slot_ref, send_ref, i, dot(turned_ref[...], active_ref[i])))


def down_third_kernel(slot_ref, active_ref, turned_ref, keep_ref):
    each(
        active_ref.shape[0],
        lambda i: put_blocks(0, slot_ref, keep_ref, i, dot(turned_ref[...], active_ref[i])),
    )


def middle_kernel(half, slot_ref, low_grad_ref, slope_ref, *rest):
    if half == 1:
        grad_ref, low_ref, up_w, down_w, out_ref, sums_ref, acc, turned = rest
        acc[...] = grad_ref[...]
        turned[...] = low_ref[...].T
    else:
        acc_ref, turned, normal_ref, inverse_ref, gain, up_w, down_w, *rest = rest
        out_ref, sums_ref, resid_ref, resid_low_ref, resid_turned_ref, acc = rest
        acc[...] = acc_ref[...]

    def step(i):
        wide = dot(low_grad_ref[...], down_w[i]) * slope_ref[i].astype(F32)
        pre_grad = wide.astype(BF16)
        sums_ref[pl.ds(3 + i, 1)] = column_sum(wide)
        put_blocks(half, slot_ref, out_ref, i, dot(turned[...], pre_grad))
        acc[...] += dot_nt(pre_grad, up_w[i])

    each(up_w.shape[0], step)
    if half == 0:
        grad_one = acc[...]
        normal = normal_ref[...]
        resid = norm_backward(grad_one, normal, inverse_ref[...], gain[...])
        resid_ref[...] = resid
        low = resid.astype(BF16)
        resid_low_ref[...] = low
        resid_turned_ref[...] = low.T
        sums_ref[0:1] = column_sum(resid)
        sums_ref[1:2] = column_sum(grad_one * normal)
        sums_ref[2:3] = column_sum(grad_one)


def attention_back_kernel(slot_ref, turned_ref, resid_ref, resid_low_ref, resid_turned_ref, *rest):
    *parts, grad_ref, sums_second, sums_first, send_ref, keep_ref, grads_ref = rest
    grad_ref[...] = resid_ref[...]
    many = len(parts) // 2
    shared = (slot_ref, turned_ref, resid_low_ref, resid_turned_ref, grad_ref, grads_ref)
    attention_back(1, *shared, *parts[:many], sums_second, send_ref)
    attention_back(0, *shared, *parts[many:], sums_first, keep_ref)


def attention_back(
    half, slot_ref, turned_ref, resid_low_ref, resid_turned_ref, grad_ref, grads_ref, sums_in_ref, qkv_ref, context_ref,
    exponent_ref, total_ref, weight, sums_ref, out_ref,
):
    cols = context_ref.shape[1]
    factor = HD**-0.5
    extra = sums_ref.shape[1]
    main = out_ref.shape[1] - 2 * extra

    def step(i):
        outer = dot(resid_low_ref[...], weight[i, :, 3 * cols :])
        totals = total_ref[i].T
        query_grads, key_grads, value_grads = [], [], []
        for h in range(cols // HD):
            at = slice(h * HD, (h + 1) * HD)
            queries, keys, values = (
                qkv_ref[i, :, part * cols + h * HD : part * cols + (h + 1) * HD] for part in range(3)
            )
            queries = queries * factor
            upstream = (outer[:, at] * totals[:, h : h + 1]).astype(BF16)
            row_term = jnp.sum(
                upstream.T.astype(F32) * context_ref[i, at].astype(F32), axis=0, keepdims=True
            )
            exponent = exponent_ref[i, h]
            prob_grad = dot_nt(values, upstream)
            score_grad = (exponent.astype(F32) * (prob_grad - row_term)).astype(BF16)
            key_grads.append(dot(score_grad, queries).astype(BF16))
            value_grads.append(dot(exponent, upstream).astype(BF16))
            query_grads.append((dot_tn(keys, score_grad) * factor).astype(BF16))
        queries = jnp.concatenate(query_grads, axis=0).T
        grads_ref[i] = jnp.concatenate([queries, *key_grads, *value_grads], axis=1)

    each(weight.shape[0], step)
    count = weight.shape[0]
    grad = jnp.concatenate([grads_ref[i] for i in range(count)], axis=1)
    grad_ref[...] += dot_nt(grad, jnp.concatenate([weight[i, :, : 3 * cols] for i in range(count)], axis=1))
    weight_grad = dot(turned_ref[...], grad)
    out_grad = dot_nt(resid_turned_ref[...], jnp.concatenate([context_ref[i] for i in range(count)], axis=0))
    columns = column_sum(grad.astype(F32))
    for i in range(count):
        put_blocks(half, slot_ref, out_ref, i, weight_grad[:, 3 * cols * i : 3 * cols * (i + 1)], slice(0, 3 * cols))
        put_blocks(half, slot_ref, out_ref, i, out_grad[:, cols * i : cols * (i + 1)], slice(3 * cols, None))
        side = jnp.concatenate([columns[:, 3 * cols * i : 3 * cols * (i + 1)], jnp.zeros((1, cols), F32)], axis=1)
        side = jnp.concatenate([sums_in_ref[i], side], axis=0)
        sums_ref[i] = side
        high = side.astype(BF16)
        low = (side - high.astype(F32)).astype(BF16)
        side = jnp.concatenate([high, low], axis=0)
        for cut in range(CUTS):
            out_ref[slot_ref[half * out_ref.shape[0] + i * CUTS + cut], main:, :] = side


def call(kernel, pieces, scalars, inputs, outs, scratch, flops, limit=16):
    whole = pl.BlockSpec(memory_space=pltpu.VMEM)
    smem = pl.BlockSpec(memory_space=pltpu.SMEM)
    return pl.pallas_call(
        kernel,
        in_specs=[smem] * len(scalars) + [whole] * len(inputs) + [whole] * len(pieces),
        out_specs=[whole] * len(outs),
        out_shape=[jax.ShapeDtypeStruct(*out) for out in outs],
        scratch_shapes=scratch,
        compiler_params=pltpu.CompilerParams(vmem_limit_bytes=limit * MIB),
        cost_estimate=pl.CostEstimate(flops=1024, bytes_accessed=1024, transcendentals=0),
    )(*scalars, *inputs, *pieces)


def shards(
    steps,
    sources,
    fsdp,
    tp,
    tokens,
    segment_ids,
    query_weight,
    key_weight,
    value_weight,
    query_bias,
    value_bias,
    output_weight,
    output_bias,
    first_gain,
    first_shift,
    up_weight,
    up_bias,
    down_weight,
    down_bias,
    second_gain,
    second_shift,
    cotangent,
):
    rows, cols = query_weight.shape
    width = rows * fsdp
    units = up_weight.shape[1]
    count = fsdp * tp
    cut_rows = width // CUTS
    blocks_n = CUTS * tp
    direct = blocks_n == count
    place = lax.axis_index("tp")
    me = lax.axis_index("fsdp") * tp + place
    doc_ids = lax.dynamic_slice_in_dim(segment_ids, place * SEQ, SEQ)

    def mine(table):
        return lax.dynamic_index_in_dim(jnp.asarray(table, jnp.int32), me, keepdims=False)

    slot_of = mine(np.argsort(sources, axis=1))
    kept = tp // 2
    if direct:
        sides = np.array(sources).reshape(count, 2, -1) % tp
        columns = np.sort(np.array([[np.unique(part) for part in parts] for parts in sides]), axis=2)
        inner = (sides[..., None] == columns[:, :, None, :]).argmax(axis=-1)
        spots = inner * CUTS + np.array(sources).reshape(count, 2, -1) // tp
        places = mine(spots.reshape(count, -1))
        slots = mine(np.argsort(spots, axis=2).reshape(count, -1))
        turns = mine(columns.reshape(count, -1))
    else:
        places = slots = jnp.tile(jnp.arange(blocks_n // 2, dtype=jnp.int32), 2)
        turns = jnp.arange(tp, dtype=jnp.int32)

    def ready(pieces):
        if direct:
            return pieces
        full = laid_out(jnp.concatenate(pieces, axis=0), slot_of, fsdp, tp)
        full = full.reshape(CUTS, cut_rows, tp, -1).transpose(2, 0, 1, 3)
        full = full.reshape(2, blocks_n // 2, cut_rows, -1)
        return [full[0], full[1]]

    def outgoing(keep, send, extra=0):
        if direct:
            return Sum(keep, send, steps, extra)
        blocks = jnp.concatenate([keep, send], axis=0)[:, :cut_rows]
        full = blocks.reshape(tp, CUTS, cut_rows, -1).transpose(1, 2, 0, 3)
        blocks = cut_up(full.reshape(fsdp, rows, -1), slot_of, fsdp, tp)
        return Sum(blocks[: count // 2], blocks[count // 2 :], steps)

    query_bias, value_bias = query_bias.reshape(tp, 1, cols), value_bias.reshape(tp, 1, cols)
    blank = jnp.zeros_like(query_bias)
    qkv_bias = jnp.concatenate([query_bias, blank, value_bias], axis=2)
    up_bias = up_bias.reshape(tp, 1, units)
    vectors = jnp.stack(
        [output_bias, first_gain, first_shift, down_bias, second_gain, second_shift]
    ).reshape(6, 1, width)
    output_bias, first_gain, first_shift, down_bias, second_gain, second_shift = (
        vectors[i] for i in range(6)
    )
    ids_row, ids_col = doc_ids.reshape(1, -1), doc_ids.reshape(-1, 1)

    a = Gather(jnp.concatenate([query_weight, key_weight, value_weight, output_weight.T], axis=1), steps)
    b = Gather(up_weight, steps)
    c = Gather(down_weight.T, steps)
    if direct:
        pair = Gather(jnp.stack([up_weight, down_weight.T]), steps)
        first = a.step()
        pair.held = after(pair.held, first)
        a_x = a.step(qkv_bias, up_bias, vectors, ids_row, ids_col)
        pair.step()
        a.held, pair.held = lax.optimization_barrier((a.held, pair.held))
        a.step()
        pair.step()
        a.held, pair.held = lax.optimization_barrier((a.held, pair.held))
        b, c = pair.split()
        a_x = a.step()
        b_z = b.step()
        a.pieces, b.held = lax.optimization_barrier((a.pieces, b.held))
        attn_w = ready(a.finish())
        b_x = b.step()
        c2 = c.held
        c_z = swap(after(c2, b_z), steps[2])
        c_x = swap(after(c2, b_z), steps[3])
    else:
        for package in (a, b, c):
            for _ in steps[:-1]:
                package.step()
        attn_w = ready(a.finish())
    many = len(attn_w) // 2
    parts = kept
    weight = ((parts, width, units), BF16)
    half = ((blocks_n // 2, cut_rows, units), BF16)
    side_half = ((blocks_n // 2, cut_rows + 16, units), BF16)
    state = pltpu.VMEM((SEQ, width), F32)
    turned = pltpu.VMEM((width, SEQ), BF16)
    mask = pltpu.VMEM((SEQ, SEQ), F32)
    wide, narrow = (SEQ, width), ((SEQ, width), BF16)
    full = (wide, F32)
    flipped = ((width, SEQ), BF16)
    flops = 2 * SEQ * width * width
    kept_outs = [weight, ((parts, SEQ, 3 * cols), BF16), ((parts, cols, SEQ), BF16),
                 ((parts, cols // HD, SEQ, SEQ), BF16), ((parts, 8, SEQ), F32)]
    common = (tokens, ids_row, ids_col, qkv_bias)
    *attn_first, acc, tokens_turned = call(
        partial(attention_kernel, 0), attn_w[:many], (places, turns), (*common, output_bias),
        [*kept_outs, full, flipped], [mask], 4 * flops,
    )
    *attn_second, normal, inverse, low = call(
        partial(attention_kernel, 1), attn_w[many:], (places, turns), (*common, acc, first_gain, first_shift),
        [*kept_outs, full, ((SEQ, 1), F32), narrow], [mask, state], 4 * flops,
    )
    if direct:
        up_w = b.finish(inverse, b_x)
        c_xz = swap(after(c_z, inverse, c_x), steps[3])
    else:
        up_w = ready(b.finish())
    outs = [weight, ((parts, SEQ, units), BF16), ((parts, SEQ, units), BF16)]
    up_first, active_first, slope_first, up_second, active_second, slope_second = call(
        up_kernel, up_w, (places, turns), (low, up_bias), outs * 2, [], 6 * flops
    )
    if direct:
        down_w = [after(piece, slope_second, c_xz) for piece in (c2, c_z, c_x, c_xz)]
        down_w = [c2, c_z, c_x, c_xz] + [swap(piece, steps[4]) for piece in down_w]
    else:
        down_w = ready(c.finish())
    down_first, acc = call(
        down_first_kernel, down_w[: len(down_w) // 2], (places,),
        (active_first, normal, first_gain, first_shift, down_bias), [weight, full], [], 2 * flops,
    )
    down_second, layer_output, grad_two, grad_low, grad_turned, down_sums, down_send = call(
        down_second_kernel, down_w[len(down_w) // 2 :], (places, slots),
        (active_second, acc, second_gain, second_shift, cotangent),
        [weight, full, full, narrow, flipped, ((8, width), F32), half], [state], 5 * flops,
    )
    (down_keep,) = call(
        down_third_kernel, [], (slots,), (active_first, grad_turned), [half], [], 2 * flops
    )
    down_sum = outgoing(down_keep, down_send)
    if direct:
        first = down_sum.step()
        down_sum.start()
        grad_low = after(grad_low, first)
    up_send, sums_second, acc, low_turned = call(
        partial(middle_kernel, 1), [up_second, down_second], (slots,),
        (grad_low, slope_second, grad_two, low), [half, ((8, width), F32), full, flipped], [], 6 * flops,
    )
    up_keep, sums_first, resid, resid_low, resid_turned = call(
        partial(middle_kernel, 0), [up_first, down_first], (slots,),
        (grad_low, slope_first, acc, low_turned, normal, inverse, first_gain),
        [half, ((8, width), F32), full, narrow, flipped], [state], 6 * flops,
    )
    up_sum = outgoing(up_keep, up_send)
    if direct:
        moved = down_sum.moved
        sent = down_sum.end()
        down_sum.start(sums_first)
        up_sum.start()
        up_sum.hold(resid_low, sent)
        first = up_sum.end()
        up_sum.start()
        resid_low = after(resid_low, first, sent)
    shared = jnp.concatenate([down_sums[:3], sums_first[:3]], axis=0)[None]

    def with_units(sums):
        return jnp.concatenate([jnp.broadcast_to(shared, (parts, 6, width)), sums[3 : 3 + parts, None]], axis=1)

    weight_second, *attn_second = attn_second
    weight_first, *attn_first = attn_first
    side_sums = ((parts, 8, units), F32)
    input_grad, side_second, side_first, attn_send, attn_keep = call(
        attention_back_kernel, [], (slots,),
        (tokens_turned, resid, resid_low, resid_turned, with_units(sums_second), *attn_second, weight_second,
         with_units(sums_first), *attn_first, weight_first),
        [full, side_sums, side_sums, side_half, side_half], [pltpu.VMEM((parts, SEQ, 3 * cols), BF16)], 20 * flops,
    )
    attn_sum = outgoing(attn_keep, attn_send, 8)
    if direct:
        attn_sum.step(*down_sum.moved, *up_sum.moved)
        down_sum.end()
        up_sum.end()
        attn_sum.start()
        up_sum.start()
        both(attn_sum, up_sum)
        pair = Sum.merge(down_sum, up_sum)
        attn_sum.start()
        pair.start()
        both(attn_sum, pair)
        attn_sum.start()
        pair.start()
        attn_sum.end()
        finals = [[part] for part in pair.end()[0]]
        attn_sum.start()
        finals.append(attn_sum.end())
    else:
        side = jnp.concatenate([side_first, side_second], axis=0)
        finals = []
        for package in (down_sum, up_sum, attn_sum):
            while package.at > 0:
                package.step()
            package.start()
            finals.append(package.end())
    if direct:
        attn_grad, side = finals[2][0][0], finals[2][1][0]
    else:
        attn_grad = finals[2][0]
        side = lax.dynamic_index_in_dim(lax.psum(side, AXES), place, keepdims=False)
    return (
        layer_output,
        input_grad,
        attn_grad[:, :cols],
        attn_grad[:, cols : 2 * cols],
        attn_grad[:, 2 * cols : 3 * cols],
        side[7, :cols],
        side[7, 2 * cols : 3 * cols],
        attn_grad[:, 3 * cols :].T,
        side[3],
        side[4],
        side[5],
        finals[1][0],
        side[6],
        finals[0][0].T,
        side[0],
        side[1],
        side[2],
    )


def solution(mesh):
    fsdp, tp = mesh.shape["fsdp"], mesh.shape["tp"]
    steps, sources = exchange_plan(fsdp, tp)
    both, up, down = P(AXES, None), P("fsdp", "tp"), P("tp", "fsdp")
    return jax.shard_map(
        partial(shards, steps, sources, fsdp, tp),
        mesh=mesh,
        in_specs=(
            both, P("fsdp"), up, up, up, P(), P(), down, P(), P(), P(), up, P(), down, P(), P(), P(), both,
        ),
        out_specs=(
            both, both, up, up, up, P("tp"), P("tp"), down, P(), P(), P(), up, P("tp"), down, P(), P(), P(),
        ),
        check_vma=False,
    )
```

profile of v0, /device:TPU:0, one launch (start us, length us, event | category | flops | bytes accessed | tf_op | source)
XLA Modules:
  0.0 211.4 jit_solution(6476893762989710641)
XLA Ops:
  0.7 0.9 copy.40
  1.5 1.0 maximum_bitcast_fusion.1
  2.5 3.1 %collective-permute-start = (bf16[1,96,768]{2,1,0:T(8,128)(2,1)S(1)}, bf16[1,96,768]{2,1,0:T(8,128)(2,1)S(1)}, u32[]{:S(2)}, u32[]{:S(2)}) collective-permute-start(bf16[1,96,768]{2,1,0:T(8,128)(2,1)S(1)} %maximum_bitcast_fusion.1), channel_id=1, source_target_pairs={{0,8},{1,17},{2,10},{3,19},{4,12},{5,21},{6,14},{7,23},{8,0},{9,25... | collective-permute-start | bytes 442376 | tf_op jit(solution)/shard_map/ppermute | solution.py:37
  5.6 0.8 reshape.167
  6.4 0.8 reshape.168
  7.2 1.0 maximum_bitcast_fusion
  8.2 1.7 collective-permute-done
  9.9 2.3 %collective-permute-start.2 = (bf16[1,2,96,768]{3,2,0,1:T(8,128)(2,1)S(1)}, bf16[1,2,96,768]{3,2,0,1:T(8,128)(2,1)S(1)}, u32[]{:S(2)}, u32[]{:S(2)}) collective-permute-start(bf16[1,2,96,768]{3,2,0,1:T(8,128)(2,1)S(1)} %maximum_bitcast_fusion), channel_id=1, source_target_pairs={{0,8},{1,17},{2,10},{3,19},{4,12},{5,21},{6,14},{7,23},{8,0},{9,25... | collective-permute-start | bytes 884744 | tf_op jit(solution)/shard_map/ppermute | solution.py:37
  12.2 0.8 dynamic_slice.17
  13.0 1.6 collective-permute-start.1
  14.6 5.4 %collective-permute-done.2 = bf16[1,2,96,768]{3,2,0,1:T(8,128)(2,1)S(1)} collective-permute-done((bf16[1,2,96,768]{3,2,0,1:T(8,128)(2,1)S(1)}, bf16[1,2,96,768]{3,2,0,1:T(8,128)(2,1)S(1)}, u32[]{:S(2)}, u32[]{:S(2)}) %collective-permute-start.2) | collective-permute-done | bytes 294944 | tf_op jit(solution)/shard_map/ppermute | solution.py:37
  20.1 2.4 %collective-permute-start.3 = (bf16[4,96,768]{2,1,0:T(8,128)(2,1)S(1)}, bf16[4,96,768]{2,1,0:T(8,128)(2,1)S(1)}, u32[]{:S(2)}, u32[]{:S(2)}) collective-permute-start(bf16[4,96,768]{2,1,0:T(8,128)(2,1)S(1)} %pad_maximum_fusion.7), channel_id=1, source_target_pairs={{0,16},{1,9},{2,18},{3,11},{4,20},{5,13},{6,22},{7,15},{8,24},{9,1... | collective-permute-start | bytes 1769480 | tf_op jit(solution)/shard_map/ppermute | solution.py:37
  22.5 1.5 collective-permute-start.4
  24.0 13.3 %collective-permute-done.3 = bf16[4,96,768]{2,1,0:T(8,128)(2,1)S(1)} collective-permute-done((bf16[4,96,768]{2,1,0:T(8,128)(2,1)S(1)}, bf16[4,96,768]{2,1,0:T(8,128)(2,1)S(1)}, u32[]{:S(2)}, u32[]{:S(2)}) %collective-permute-start.3) | collective-permute-done | bytes 589856 | tf_op jit(solution)/shard_map/ppermute | solution.py:37
  37.5 1.8 collective-permute-start.5
  39.3 0.9 slice_bitcast_fusion
  40.3 17.1 %collective-permute-done.6 = bf16[4,96,768]{2,1,0:T(8,128)(2,1)S(1)} collective-permute-done((bf16[4,96,768]{2,1,0:T(8,128)(2,1)S(1)}, bf16[4,96,768]{2,1,0:T(8,128)(2,1)S(1)}, u32[]{:S(2)}, u32[]{:S(2)}) %collective-permute-start.6) | collective-permute-done | bytes 589856 | tf_op jit(solution)/shard_map/ppermute | solution.py:37
  58.6 0.7 fusion.31.place_ref
  60.0 1.7 collective-permute-start.13
  61.7 7.6 %shard_map.332 = (bf16[2,768,768]{2,1,0:T(8,128)(2,1)S(1)}, bf16[2,512,576]{2,1,0:T(8,128)(2,1)S(1)}, bf16[2,192,512]{2,1,0:T(8,128)(2,1)S(1)}, bf16[2,3,512,512...) custom-call(s32[32]{0:T(128)S(1)} %fusion.31.place_ref, ...), custom_call_target="tpu_custom_call" | custom-call | flops 1024 | bytes 1024 | tf_op jit(solution)/shard_map/pallas_call | solution.py:435
  69.4 8.7 %shard_map.333 = (bf16[2,768,768]{2,1,0:T(8,128)(2,1)S(1)}, bf16[2,512,576]{2,1,0:T(8,128)(2,1)S(1)}, bf16[2,192,512]{2,1,0:T(8,128)(2,1)S(1)}, bf16[2,3,512,512...) custom-call(s32[32]{0:T(128)S(1)} %fusion.31.place_ref, ...), custom_call_target="tpu_custom_call" | custom-call | flops 1024 | bytes 1024 | tf_op jit(solution)/shard_map/pallas_call | solution.py:435
  78.7 1.9 collective-permute-done.13.rest_2_
  80.9 1.0 collective-permute-done.10.rest_2_
  82.0 1.0 collective-permute-done.11.rest_3_
  83.0 6.9 %shard_map.334 = (bf16[2,768,768]{2,1,0:T(8,128)(2,1)S(1)}, bf16[2,512,768]{2,1,0:T(8,128)(2,1)S(1)}, bf16[2,512,768]{2,1,0:T(8,128)(2,1)S(1)}, bf16[2,768,768]{...) custom-call(s32[32]{0:T(128)S(1)} %fusion.31.place_ref, ...), custom_call_target="tpu_custom_call" | custom-call | flops 1024 | bytes 1024 | tf_op jit(solution)/shard_map/pallas_call | solution.py:435
  92.2 2.7 %shard_map.335 = (bf16[2,768,768]{2,1,0:T(8,128)(2,1)S(1)}, f32[512,768]{1,0:T(8,128)S(1)}) custom-call(s32[32]{0:T(128)S(1)} %fusion.31.place_ref, bf16[2,512,768]{2,1,0:T(8,128)(2,1)S(1)} %get-tuple-element.101.active_ref, f32[512,768]{1,0:T(8,128)S(1)} %get-tuple-element.102.normal_ref.rest_2_, f32[1,768]{1,0:T(1,128)S(1)} %stack.50.rest_1_.first_gain.rest_4_, ...), custom_call_target="tpu_custom_call" | custom-call | flops 1024 | bytes 1024 | tf_op jit(solution)/shard_map/pallas_call | solution.py:435
  95.0 6.2 %shard_map.336 = (bf16[2,768,768]{2,1,0:T(8,128)(2,1)S(1)}, f32[512,768]{1,0:T(8,128)}, f32[512,768]{1,0:T(8,128)S(1)}, bf16[512,768]{1,0:T(8,128)(2,1)S(1)}, bf...) custom-call(s32[32]{0:T(128)S(1)} %fusion.31.place_ref, ...), custom_call_target="tpu_custom_call" | custom-call | flops 1024 | bytes 1024 | tf_op jit(solution)/shard_map/pallas_call | solution.py:435
  102.0 2.1 shard_map.337
  104.3 1.7 collective-permute-done.19
  107.1 5.0 %shard_map.338 = (bf16[16,96,768]{2,1,0:T(8,128)(2,1)S(1)}, f32[8,768]{1,0:T(8,128)S(1)}, f32[512,768]{1,0:T(8,128)S(1)}, bf16[768,512]{1,0:T(8,128)(2,1)S(1)}) custom-call(s32[32]{0:T(128)S(1)} %fusion.32.slot_ref, bf16[512,768]{1,0:T(8,128)(2,1)S(1)} %get-tuple-element.116.low_grad_ref, bf16[2,512,768]{2,1,0:T(8,128)(2,1)S(1)} %get-tuple-element.106.slope_ref, ...), custom_call_target="tpu_custom_call" | custom-call | flops 1024 | bytes 1024 | tf_op jit(solution)/shard_map/pallas_call | solution.py:435
  112.3 1.1 collective-permute-start.21
  113.4 5.8 %shard_map.339 = (bf16[16,96,768]{2,1,0:T(8,128)(2,1)S(1)}, f32[8,768]{1,0:T(8,128)S(1)}, f32[512,768]{1,0:T(8,128)S(1)}, bf16[512,768]{1,0:T(8,128)(2,1)S(1)}, bf16[768,512]{1,0:T(8,128)(2,1)S(1)}) custom-call(s32[32]{0:T(128)S(1)} %fusion.32.slot_ref, bf16[512,768]{1,0:T(8,128)(2,1)S(1)} %get-tuple-element.116.low_grad_ref, ...), custom_call_target="tpu_custom_call" | custom-call | flops 1024 | bytes 1024 | tf_op jit(solution)/shard_map/pallas_call | solution.py:435
  119.2 3.8 %collective-permute-done.23 = bf16[8,96,768]{2,1,0:T(8,128)(2,1)S(1)} collective-permute-done((bf16[8,96,768]{2,1,0:T(8,128)(2,1)S(1)}, bf16[8,96,768]{2,1,0:T(8,128)(2,1)S(1)}, u32[]{:S(2)}, u32[]{:S(2)}) %collective-permute-start.23) | collective-permute-done | bytes 1179680 | tf_op jit(solution)/shard_map/ppermute | solution.py:37
  123.4 0.7 add_convert_fusion
  124.5 2.4 %collective-permute-start.24 = (bf16[4,96,768]{2,1,0:T(8,128)(2,1)S(1)}, bf16[4,96,768]{2,1,0:T(8,128)(2,1)S(1)}, u32[]{:S(2)}, u32[]{:S(2)}) collective-permute-start(bf16[4,96,768]{2,1,0:T(8,128)(2,1)S(1)} %get-tuple-element.148), channel_id=1, source_target_pairs={{0,16},{1,9},{2,18},{3,11},{4,20},{5,13},{6,22},{7,15},{8,24},{9,1... | collective-permute-start | bytes 1769480 | tf_op jit(solution)/shard_map/ppermute | solution.py:37
  127.0 16.8 %shard_map.340 = (f32[512,768]{1,0:T(8,128)}, f32[2,8,768]{2,1,0:T(8,128)}, f32[2,8,768]{2,1,0:T(8,128)}, bf16[16,112,768]{2,1,0:T(8,128)(2,1)S(1)}, bf16[16,112,768]{2,1,0:T(8,128)(2,1)S(1)}) custom-call(s32[32]{0:T(128)S(1)} %fusion.32.slot_ref, bf16[768,512]{1,0:T(8,128)(2,1)S(1)} %get-tuple-element.112.turned_ref, ...), custom_call_target="tpu_custom_call" | custom-call | flops 1024 | bytes 1024 | tf_op jit(solution)/shard_map/pallas_call | solution.py:435
  145.3 2.0 collective-permute-done.27
  148.1 1.8 collective-permute-start.28
  151.6 15.7 %collective-permute-done.29 = bf16[4,96,768]{2,1,0:T(8,128)(2,1)S(1)} collective-permute-done((bf16[4,96,768]{2,1,0:T(8,128)(2,1)S(1)}, bf16[4,96,768]{2,1,0:T(8,128)(2,1)S(1)}, u32[]{:S(2)}, u32[]{:S(2)}) %collective-permute-start.29) | collective-permute-done | bytes 589856 | tf_op jit(solution)/shard_map/ppermute | solution.py:37
  168.7 1.6 collective-permute-start.31
  170.5 8.2 %collective-permute-done.31 = bf16[2,2,96,768]{3,2,0,1:T(8,128)(2,1)S(1)} collective-permute-done((bf16[2,2,96,768]{3,2,0,1:T(8,128)(2,1)S(1)}, bf16[2,2,96,768]{3,2,0,1:T(8,128)(2,1)S(1)}, u32[]{:S(2)}, u32[]{:S(2)}) %collective-permute-start.31) | collective-permute-done | bytes 589856 | tf_op jit(solution)/shard_map/ppermute | solution.py:37
  178.7 13.9 %collective-permute-done.30 = bf16[4,112,768]{2,1,0:T(8,128)(2,1)S(1)} collective-permute-done((bf16[4,112,768]{2,1,0:T(8,128)(2,1)S(1)}, bf16[4,112,768]{2,1,0:T(8,128)(2,1)S(1)}, u32[]{:S(2)}, u32[]{:S(2)}) %collective-permute-start.30) | collective-permute-done | bytes 688160 | tf_op jit(solution)/shard_map/ppermute | solution.py:37
  193.0 1.4 collective-permute-start.32
  194.5 7.0 %collective-permute-done.34 = bf16[1,2,96,768]{3,2,0,1:T(8,128)(2,1)S(1)} collective-permute-done((bf16[1,2,96,768]{3,2,0,1:T(8,128)(2,1)S(1)}, bf16[1,2,96,768]{3,2,0,1:T(8,128)(2,1)S(1)}, u32[]{:S(2)}, u32[]{:S(2)}) %collective-permute-start.34) | collective-permute-done | bytes 294944 | tf_op jit(solution)/shard_map/ppermute | solution.py:37
  201.6 0.8 slice_bitcast_fusion.2
  202.8 5.3 %collective-permute-done.33 = bf16[1,112,768]{2,1,0:T(8,128)(2,1)S(1)} collective-permute-done((bf16[1,112,768]{2,1,0:T(8,128)(2,1)S(1)}, bf16[1,112,768]{2,1,0:T(8,128)(2,1)S(1)}, u32[]{:S(2)}, u32[]{:S(2)}) %collective-permute-start.33) | collective-permute-done | bytes 172064 | tf_op jit(solution)/shard_map/ppermute | solution.py:37
  209.5 0.8 slice_bitcast_fusion.4
  210.2 0.7 copy.43
  (165 shorter events, 16.4 us)
Async XLA Ops:
  2.5 7.4 %collective-permute-start = (bf16[1,96,768]{2,1,0:T(8,128)(2,1)S(1)}, bf16[1,96,768]{2,1,0:T(8,128)(2,1)S(1)}, u32[]{:S(2)}, u32[]{:S(2)}) collective-permute-start(bf16[1,96,768]{2,1,0:T(8,128)(2,1)S(1)} %maximum_bitcast_fusion.1), channel_id=1, source_target_pairs={{0,8},{1,17},{2,10},{3,19},{4,12},{5,21},{6,14},{7,23},{8,0},{9,25... | collective-permute-start | bytes 442376 | tf_op jit(solution)/shard_map/ppermute | solution.py:37
  9.9 10.0 %collective-permute-start.2 = (bf16[1,2,96,768]{3,2,0,1:T(8,128)(2,1)S(1)}, bf16[1,2,96,768]{3,2,0,1:T(8,128)(2,1)S(1)}, u32[]{:S(2)}, u32[]{:S(2)}) collective-permute-start(bf16[1,2,96,768]{3,2,0,1:T(8,128)(2,1)S(1)} %maximum_bitcast_fusion), channel_id=1, source_target_pairs={{0,8},{1,17},{2,10},{3,19},{4,12},{5,21},{6,14},{7,23},{8,0},{9,25... | collective-permute-start | bytes 884744 | tf_op jit(solution)/shard_map/ppermute | solution.py:37
  13.0 7.0 %collective-permute-start.1 = (bf16[2,96,768]{2,1,0:T(8,128)(2,1)S(1)}, bf16[2,96,768]{2,1,0:T(8,128)(2,1)S(1)}, u32[]{:S(2)}, u32[]{:S(2)}) collective-permute-start(bf16[2,96,768]{2,1,0:T(8,128)(2,1)S(1)} %pad_maximum_fusion.13), channel_id=1, source_target_pairs={{0,4},{1,3},{2,6},{3,1},{4,0},{5,7},{6,2},{7,5},{8,12},{9,11},{10,... | collective-permute-start | bytes 884744 | tf_op jit(solution)/shard_map/ppermute | solution.py:37
  20.1 17.2 %collective-permute-start.3 = (bf16[4,96,768]{2,1,0:T(8,128)(2,1)S(1)}, bf16[4,96,768]{2,1,0:T(8,128)(2,1)S(1)}, u32[]{:S(2)}, u32[]{:S(2)}) collective-permute-start(bf16[4,96,768]{2,1,0:T(8,128)(2,1)S(1)} %pad_maximum_fusion.7), channel_id=1, source_target_pairs={{0,16},{1,9},{2,18},{3,11},{4,20},{5,13},{6,22},{7,15},{8,24},{9,1... | collective-permute-start | bytes 1769480 | tf_op jit(solution)/shard_map/ppermute | solution.py:37
  22.5 14.9 %collective-permute-start.4 = (bf16[2,2,96,768]{3,2,0,1:T(8,128)(2,1)S(1)}, bf16[2,2,96,768]{3,2,0,1:T(8,128)(2,1)S(1)}, u32[]{:S(2)}, u32[]{:S(2)}) collective-permute-start(bf16[2,2,96,768]{3,2,0,1:T(8,128)(2,1)S(1)} %pad_maximum_fusion.8), channel_id=1, source_target_pairs={{0,4},{1,3},{2,6},{3,1},{4,0},{5,7},{6,2},{7,5},{8,12},{9,11},{10,... | collective-permute-start | bytes 1769480 | tf_op jit(solution)/shard_map/ppermute | solution.py:37
  37.5 19.9 %collective-permute-start.5 = (bf16[8,96,768]{2,1,0:T(8,128)(2,1)S(1)}, bf16[8,96,768]{2,1,0:T(8,128)(2,1)}, u32[]{:S(2)}, u32[]{:S(2)}) collective-permute-start(bf16[8,96,768]{2,1,0:T(8,128)(2,1)S(1)} %pad_maximum_fusion.2.rest_1_), channel_id=1, source_target_pairs={{0,2},{1,5},{2,0},{3,7},{4,6},{5,1},{6,4},{7,3},{8,10},{9,13},{10,... | collective-permute-start | bytes 3538952 | tf_op jit(solution)/shard_map/ppermute | solution.py:37
  40.2 18.4 %copy-start.14 = (f32[768]{0:T(1024)S(1)}, f32[768]{0:T(1024)}, u32[]{:S(2)}) copy-start(f32[768]{0:T(1024)} %param.30) | copy-start | bytes 9220
  40.2 18.4 %copy-start.15 = (f32[768]{0:T(1024)S(1)}, f32[768]{0:T(1024)}, u32[]{:S(2)}) copy-start(f32[768]{0:T(1024)} %param.31) | copy-start | bytes 9220
  40.2 18.4 %copy-start.16 = (f32[768]{0:T(1024)S(1)}, f32[768]{0:T(1024)}, u32[]{:S(2)}) copy-start(f32[768]{0:T(1024)} %param.29) | copy-start | bytes 9220
  40.2 21.5 %copy-start = (bf16[512,768]{1,0:T(8,128)(2,1)S(1)}, bf16[512,768]{1,0:T(8,128)(2,1)}, u32[]{:S(2)}) copy-start(bf16[512,768]{1,0:T(8,128)(2,1)} %tokens_ref.3) | copy-start | bytes 2359300
  40.2 17.2 %collective-permute-start.6 = (bf16[4,96,768]{2,1,0:T(8,128)(2,1)S(1)}, bf16[4,96,768]{2,1,0:T(8,128)(2,1)S(1)}, u32[]{:S(2)}, u32[]{:S(2)}) collective-permute-start(bf16[4,96,768]{2,1,0:T(8,128)(2,1)S(1)} %get-tuple-element.237), channel_id=1, source_target_pairs={{0,16},{1,9},{2,18},{3,11},{4,20},{5,13},{6,22},{7,15},{8,24},{9,1... | collective-permute-start | bytes 1769480 | tf_op jit(solution)/shard_map/ppermute | solution.py:37
  57.5 11.9 %collective-permute-start.7 = (bf16[8,96,768]{2,1,0:T(8,128)(2,1)S(1)}, bf16[8,96,768]{2,1,0:T(8,128)(2,1)}, u32[]{:S(2)}, u32[]{:S(2)}) collective-permute-start(bf16[8,96,768]{2,1,0:T(8,128)(2,1)S(1)} %pad_maximum_fusion.2.rest_1_), channel_id=1, source_target_pairs={{0,1},{1,0},{2,3},{3,2},{4,5},{5,4},{6,7},{7,6},{8,9},{9,8},{10,11... | collective-permute-start | bytes 3538952 | tf_op jit(solution)/shard_map/ppermute | solution.py:37
  57.6 11.8 %collective-permute-start.8 = (bf16[8,96,768]{2,1,0:T(8,128)(2,1)}, bf16[8,96,768]{2,1,0:T(8,128)(2,1)}, u32[]{:S(2)}, u32[]{:S(2)}) collective-permute-start(bf16[8,96,768]{2,1,0:T(8,128)(2,1)} %collective-permute-done.5.rest_2_), channel_id=1, source_target_pairs={{0,1},{1,0},{2,3},{3,2},{4,5},{5,4},{6,7},{7,6},{8,9},{9,8},{10,11... | collective-permute-start | bytes 3538952 | tf_op jit(solution)/shard_map/ppermute | solution.py:37
  58.1 20.1 %collective-permute-start.9 = (bf16[8,96,768]{2,1,0:T(8,128)(2,1)S(1)}, bf16[8,96,768]{2,1,0:T(8,128)(2,1)}, u32[]{:S(2)}, u32[]{:S(2)}) collective-permute-start(bf16[8,96,768]{2,1,0:T(8,128)(2,1)S(1)} %pad_maximum_fusion.4.rest_0_), channel_id=1, source_target_pairs={{0,2},{1,5},{2,0},{3,7},{4,6},{5,1},{6,4},{7,3},{8,10},{9,13},{10,... | collective-permute-start | bytes 3538952 | tf_op jit(solution)/shard_map/ppermute | solution.py:37
  60.0 20.6 %collective-permute-start.13 = (bf16[4,96,768]{2,1,0:T(8,128)(2,1)}, bf16[4,96,768]{2,1,0:T(8,128)(2,1)S(1)}, u32[]{:S(2)}, u32[]{:S(2)}) collective-permute-start(bf16[4,96,768]{2,1,0:T(8,128)(2,1)} %get-tuple-element.107.rest_0_), channel_id=1, source_target_pairs={{0,2},{1,5},{2,0},{3,7},{4,6},{5,1},{6,4},{7,3},{8,10},{9,13},{10,... | collective-permute-start | bytes 1769480 | tf_op jit(solution)/shard_map/ppermute | solution.py:37
  61.7 18.9 %collective-permute-start.12 = (bf16[4,96,768]{2,1,0:T(8,128)(2,1)}, bf16[4,96,768]{2,1,0:T(8,128)(2,1)S(1)}, u32[]{:S(2)}, u32[]{:S(2)}) collective-permute-start(bf16[4,96,768]{2,1,0:T(8,128)(2,1)} %get-tuple-element.107.rest_0_), channel_id=1, source_target_pairs={{0,16},{1,9},{2,18},{3,11},{4,20},{5,13},{6,22},{7,15},{8,24},{9,1... | collective-permute-start | bytes 1769480 | tf_op jit(solution)/shard_map/ppermute | solution.py:37
  69.4 8.7 %copy-start.2 = (bf16[2,512,576]{2,1,0:T(8,128)(2,1)}, bf16[2,512,576]{2,1,0:T(8,128)(2,1)S(1)}, u32[]{:S(2)}) copy-start(bf16[2,512,576]{2,1,0:T(8,128)(2,1)S(1)} %get-tuple-element.140.rest_7_) | copy-start | bytes 3538948
  69.4 8.7 %copy-start.7 = (bf16[2,192,512]{2,1,0:T(8,128)(2,1)}, bf16[2,192,512]{2,1,0:T(8,128)(2,1)S(1)}, u32[]{:S(2)}) copy-start(bf16[2,192,512]{2,1,0:T(8,128)(2,1)S(1)} %get-tuple-element.141.rest_8_) | copy-start | bytes 1179652
  69.4 13.6 %copy-start.13 = (f32[3072]{0:T(1024)S(1)}, f32[3072]{0:T(1024)}, u32[]{:S(2)}) copy-start(f32[3072]{0:T(1024)} %param.33) | copy-start | bytes 36868
  78.1 11.8 %copy-start.4 = (bf16[2,512,576]{2,1,0:T(8,128)(2,1)}, bf16[2,512,576]{2,1,0:T(8,128)(2,1)S(1)}, u32[]{:S(2)}) copy-start(bf16[2,512,576]{2,1,0:T(8,128)(2,1)S(1)} %get-tuple-element.135.rest_1_) | copy-start | bytes 3538948
  78.1 11.8 %copy-start.9 = (bf16[2,192,512]{2,1,0:T(8,128)(2,1)}, bf16[2,192,512]{2,1,0:T(8,128)(2,1)S(1)}, u32[]{:S(2)}) copy-start(bf16[2,192,512]{2,1,0:T(8,128)(2,1)S(1)} %get-tuple-element.136.rest_2_) | copy-start | bytes 1179652
  78.1 11.8 %copy-start.11 = (f32[512,1]{1,0:T(8,128)}, f32[512,1]{1,0:T(8,128)S(1)}, u32[]{:S(2)}) copy-start(f32[512,1]{1,0:T(8,128)S(1)} %get-tuple-element.97.rest_3_) | copy-start | bytes 6148
  78.1 3.8 %collective-permute-start.10 = (bf16[8,96,768]{2,1,0:T(8,128)(2,1)S(1)}, bf16[8,96,768]{2,1,0:T(8,128)(2,1)S(1)}, u32[]{:S(2)}, u32[]{:S(2)}) collective-permute-start(bf16[8,96,768]{2,1,0:T(8,128)(2,1)S(1)} %pad_maximum_fusion.4.rest_0_), channel_id=1, source_target_pairs={{0,1},{1,0},{2,3},{3,2},{4,5},{5,4},{6,7},{7,6},{8,9},{9,8},{10,11... | collective-permute-start | bytes 3538952 | tf_op jit(solution)/shard_map/ppermute | solution.py:37
  78.2 4.7 %collective-permute-start.11 = (bf16[8,96,768]{2,1,0:T(8,128)(2,1)}, bf16[8,96,768]{2,1,0:T(8,128)(2,1)S(1)}, u32[]{:S(2)}, u32[]{:S(2)}) collective-permute-start(bf16[8,96,768]{2,1,0:T(8,128)(2,1)} %collective-permute-done.9.rest_1_), channel_id=1, source_target_pairs={{0,1},{1,0},{2,3},{3,2},{4,5},{5,4},{6,7},{7,6},{8,9},{9,8},{10,11... | collective-permute-start | bytes 3538952 | tf_op jit(solution)/shard_map/ppermute | solution.py:37
  80.6 9.9 %collective-permute-start.14 = (bf16[4,96,768]{2,1,0:T(8,128)(2,1)S(1)}, bf16[4,96,768]{2,1,0:T(8,128)(2,1)S(1)}, u32[]{:S(2)}, u32[]{:S(2)}) collective-permute-start(bf16[4,96,768]{2,1,0:T(8,128)(2,1)S(1)} %collective-permute-done.12.rest_1_), channel_id=1, source_target_pairs={{0,2},{1,5},{2,0},{3,7},{4,6},{5,1},{6,4},{7,3},{8,10},{9,13},{10,... | collective-permute-start | bytes 1769480 | tf_op jit(solution)/shard_map/ppermute | solution.py:37
  83.0 8.5 %copy-start.17 = (f32[768]{0:T(1024)S(1)}, f32[768]{0:T(1024)}, u32[]{:S(2)}) copy-start(f32[768]{0:T(1024)} %param.35) | copy-start | bytes 9220
  83.0 8.5 %copy-start.18 = (f32[768]{0:T(1024)S(1)}, f32[768]{0:T(1024)}, u32[]{:S(2)}) copy-start(f32[768]{0:T(1024)} %param.36) | copy-start | bytes 9220
  83.0 8.6 %copy-start.19 = (f32[768]{0:T(1024)S(1)}, f32[768]{0:T(1024)}, u32[]{:S(2)}) copy-start(f32[768]{0:T(1024)} %param.37) | copy-start | bytes 9220
  90.5 4.5 %collective-permute-start.15 = (bf16[4,96,768]{2,1,0:T(8,128)(2,1)S(1)}, bf16[4,96,768]{2,1,0:T(8,128)(2,1)S(1)}, u32[]{:S(2)}, u32[]{:S(2)}) collective-permute-start(bf16[4,96,768]{2,1,0:T(8,128)(2,1)S(1)} %copy-done.1), channel_id=1, source_target_pairs={{0,1},{1,0},{2,3},{3,2},{4,5},{5,4},{6,7},{7,6},{8,9},{9,8},{10,11... | collective-permute-start | bytes 1769480 | tf_op jit(solution)/shard_map/ppermute | solution.py:37
  90.5 4.5 %collective-permute-start.16 = (bf16[4,96,768]{2,1,0:T(8,128)(2,1)S(1)}, bf16[4,96,768]{2,1,0:T(8,128)(2,1)S(1)}, u32[]{:S(2)}, u32[]{:S(2)}) collective-permute-start(bf16[4,96,768]{2,1,0:T(8,128)(2,1)S(1)} %collective-permute-done.12.rest_1_), channel_id=1, source_target_pairs={{0,1},{1,0},{2,3},{3,2},{4,5},{5,4},{6,7},{7,6},{8,9},{9,8},{10,11... | collective-permute-start | bytes 1769480 | tf_op jit(solution)/shard_map/ppermute | solution.py:37
  91.0 4.0 %collective-permute-start.17 = (bf16[4,96,768]{2,1,0:T(8,128)(2,1)S(1)}, bf16[4,96,768]{2,1,0:T(8,128)(2,1)S(1)}, u32[]{:S(2)}, u32[]{:S(2)}) collective-permute-start(bf16[4,96,768]{2,1,0:T(8,128)(2,1)S(1)} %collective-permute-done.13.rest_2_), channel_id=1, source_target_pairs={{0,1},{1,0},{2,3},{3,2},{4,5},{5,4},{6,7},{7,6},{8,9},{9,8},{10,11... | collective-permute-start | bytes 1769480 | tf_op jit(solution)/shard_map/ppermute | solution.py:37
  91.0 4.0 %collective-permute-start.18 = (bf16[4,96,768]{2,1,0:T(8,128)(2,1)S(1)}, bf16[4,96,768]{2,1,0:T(8,128)(2,1)S(1)}, u32[]{:S(2)}, u32[]{:S(2)}) collective-permute-start(bf16[4,96,768]{2,1,0:T(8,128)(2,1)S(1)} %collective-permute-done.14.rest_3_), channel_id=1, source_target_pairs={{0,1},{1,0},{2,3},{3,2},{4,5},{5,4},{6,7},{7,6},{8,9},{9,8},{10,11... | collective-permute-start | bytes 1769480 | tf_op jit(solution)/shard_map/ppermute | solution.py:37
  101.4 2.9 %collective-permute-start.22 = (bf16[8,96,768]{2,1,0:T(8,128)(2,1)S(1)}, bf16[8,96,768]{2,1,0:T(8,128)(2,1)S(1)}, u32[]{:S(2)}, u32[]{:S(2)}) collective-permute-start(bf16[8,96,768]{2,1,0:T(8,128)(2,1)S(1)} %get-tuple-element.224), channel_id=1, source_target_pairs={{0,1},{1,0},{2,3},{3,2},{4,5},{5,4},{6,7},{7,6},{8,9},{9,8},{10,11... | collective-permute-start | bytes 3538952 | tf_op jit(solution)/shard_map/ppermute | solution.py:37
  101.6 4.4 %collective-permute-start.19 = (bf16[8,96,768]{2,1,0:T(8,128)(2,1)S(1)}, bf16[8,96,768]{2,1,0:T(8,128)(2,1)S(1)}, u32[]{:S(2)}, u32[]{:S(2)}) collective-permute-start(bf16[8,96,768]{2,1,0:T(8,128)(2,1)S(1)} %get-tuple-element.225), channel_id=1, source_target_pairs={{0,1},{1,0},{2,3},{3,2},{4,5},{5,4},{6,7},{7,6},{8,9},{9,8},{10,11... | collective-permute-start | bytes 3538952 | tf_op jit(solution)/shard_map/ppermute | solution.py:37
  106.7 16.3 %collective-permute-start.23 = (bf16[8,96,768]{2,1,0:T(8,128)(2,1)S(1)}, bf16[8,96,768]{2,1,0:T(8,128)(2,1)S(1)}, u32[]{:S(2)}, u32[]{:S(2)}) collective-permute-start(bf16[8,96,768]{2,1,0:T(8,128)(2,1)S(1)} %get-tuple-element.223), channel_id=1, source_target_pairs={{0,2},{1,5},{2,0},{3,7},{4,6},{5,1},{6,4},{7,3},{8,10},{9,13},{10,... | collective-permute-start | bytes 3538952 | tf_op jit(solution)/shard_map/ppermute | solution.py:37
  112.3 11.0 %collective-permute-start.21 = (bf16[8,96,768]{2,1,0:T(8,128)(2,1)S(1)}, bf16[8,96,768]{2,1,0:T(8,128)(2,1)S(1)}, u32[]{:S(2)}, u32[]{:S(2)}) collective-permute-start(bf16[8,96,768]{2,1,0:T(8,128)(2,1)S(1)} %get-tuple-element.226), channel_id=1, source_target_pairs={{0,1},{1,0},{2,3},{3,2},{4,5},{5,4},{6,7},{7,6},{8,9},{9,8},{10,11... | collective-permute-start | bytes 3538952 | tf_op jit(solution)/shard_map/ppermute | solution.py:37
  113.4 9.9 %collective-permute-start.20 = (bf16[8,96,768]{2,1,0:T(8,128)(2,1)S(1)}, bf16[8,96,768]{2,1,0:T(8,128)(2,1)S(1)}, u32[]{:S(2)}, u32[]{:S(2)}) collective-permute-start(bf16[8,96,768]{2,1,0:T(8,128)(2,1)S(1)} %get-tuple-element.227), channel_id=1, source_target_pairs={{0,1},{1,0},{2,3},{3,2},{4,5},{5,4},{6,7},{7,6},{8,9},{9,8},{10,11... | collective-permute-start | bytes 3538952 | tf_op jit(solution)/shard_map/ppermute | solution.py:37
  124.1 19.8 %collective-permute-start.25 = (bf16[8,96,768]{2,1,0:T(8,128)(2,1)S(1)}, bf16[8,96,768]{2,1,0:T(8,128)(2,1)S(1)}, u32[]{:S(2)}, u32[]{:S(2)}) collective-permute-start(bf16[8,96,768]{2,1,0:T(8,128)(2,1)S(1)} %get-tuple-element.221), channel_id=1, source_target_pairs={{0,2},{1,5},{2,0},{3,7},{4,6},{5,1},{6,4},{7,3},{8,10},{9,13},{10,... | collective-permute-start | bytes 3538952 | tf_op jit(solution)/shard_map/ppermute | solution.py:37
  124.5 19.4 %collective-permute-start.24 = (bf16[4,96,768]{2,1,0:T(8,128)(2,1)S(1)}, bf16[4,96,768]{2,1,0:T(8,128)(2,1)S(1)}, u32[]{:S(2)}, u32[]{:S(2)}) collective-permute-start(bf16[4,96,768]{2,1,0:T(8,128)(2,1)S(1)} %get-tuple-element.148), channel_id=1, source_target_pairs={{0,16},{1,9},{2,18},{3,11},{4,20},{5,13},{6,22},{7,15},{8,24},{9,1... | collective-permute-start | bytes 1769480 | tf_op jit(solution)/shard_map/ppermute | solution.py:37
  144.1 3.2 %collective-permute-start.27 = (bf16[8,112,768]{2,1,0:T(8,128)(2,1)S(1)}, bf16[8,112,768]{2,1,0:T(8,128)(2,1)S(1)}, u32[]{:S(2)}, u32[]{:S(2)}) collective-permute-start(bf16[8,112,768]{2,1,0:T(8,128)(2,1)S(1)} %get-tuple-element.215), channel_id=1, source_target_pairs={{0,1},{1,0},{2,3},{3,2},{4,5},{5,4},{6,7},{7,6},{8,9},{9,8},{10,11... | collective-permute-start | bytes 4128776 | tf_op jit(solution)/shard_map/ppermute | solution.py:37
  144.7 6.0 %collective-permute-start.26 = (bf16[8,112,768]{2,1,0:T(8,128)(2,1)S(1)}, bf16[8,112,768]{2,1,0:T(8,128)(2,1)S(1)}, u32[]{:S(2)}, u32[]{:S(2)}) collective-permute-start(bf16[8,112,768]{2,1,0:T(8,128)(2,1)S(1)} %get-tuple-element.214), channel_id=1, source_target_pairs={{0,1},{1,0},{2,3},{3,2},{4,5},{5,4},{6,7},{7,6},{8,9},{9,8},{10,11... | collective-permute-start | bytes 4128776 | tf_op jit(solution)/shard_map/ppermute | solution.py:37
  148.1 19.2 %collective-permute-start.28 = (bf16[8,112,768]{2,1,0:T(8,128)(2,1)S(1)}, bf16[8,112,768]{2,1,0:T(8,128)(2,1)S(1)}, u32[]{:S(2)}, u32[]{:S(2)}) collective-permute-start(bf16[8,112,768]{2,1,0:T(8,128)(2,1)S(1)} %pad_maximum_fusion.1), channel_id=1, source_target_pairs={{0,2},{1,5},{2,0},{3,7},{4,6},{5,1},{6,4},{7,3},{8,10},{9,13},{10,... | collective-permute-start | bytes 4128776 | tf_op jit(solution)/shard_map/ppermute | solution.py:37
  150.2 17.1 %collective-permute-start.29 = (bf16[4,96,768]{2,1,0:T(8,128)(2,1)S(1)}, bf16[4,96,768]{2,1,0:T(8,128)(2,1)S(1)}, u32[]{:S(2)}, u32[]{:S(2)}) collective-permute-start(bf16[4,96,768]{2,1,0:T(8,128)(2,1)S(1)} %get-tuple-element.219), channel_id=1, source_target_pairs={{0,16},{1,9},{2,18},{3,11},{4,20},{5,13},{6,22},{7,15},{8,24},{9,1... | collective-permute-start | bytes 1769480 | tf_op jit(solution)/shard_map/ppermute | solution.py:37
  168.3 24.2 %collective-permute-start.30 = (bf16[4,112,768]{2,1,0:T(8,128)(2,1)S(1)}, bf16[4,112,768]{2,1,0:T(8,128)(2,1)S(1)}, u32[]{:S(2)}, u32[]{:S(2)}) collective-permute-start(bf16[4,112,768]{2,1,0:T(8,128)(2,1)S(1)} %pad_maximum_fusion.6), channel_id=1, source_target_pairs={{0,16},{1,9},{2,18},{3,11},{4,20},{5,13},{6,22},{7,15},{8,24},{9,1... | collective-permute-start | bytes 2064392 | tf_op jit(solution)/shard_map/ppermute | solution.py:37
  168.7 9.9 %collective-permute-start.31 = (bf16[2,2,96,768]{3,2,0,1:T(8,128)(2,1)S(1)}, bf16[2,2,96,768]{3,2,0,1:T(8,128)(2,1)S(1)}, u32[]{:S(2)}, u32[]{:S(2)}) collective-permute-start(bf16[2,2,96,768]{3,2,0,1:T(8,128)(2,1)S(1)} %pad_maximum_fusion.9), channel_id=1, source_target_pairs={{0,4},{1,3},{2,6},{3,1},{4,0},{5,7},{6,2},{7,5},{8,12},{9,11},{10,... | collective-permute-start | bytes 1769480 | tf_op jit(solution)/shard_map/ppermute | solution.py:37
  192.9 8.6 %collective-permute-start.34 = (bf16[1,2,96,768]{3,2,0,1:T(8,128)(2,1)S(1)}, bf16[1,2,96,768]{3,2,0,1:T(8,128)(2,1)S(1)}, u32[]{:S(2)}, u32[]{:S(2)}) collective-permute-start(bf16[1,2,96,768]{3,2,0,1:T(8,128)(2,1)S(1)} %add_convert_fusion.8), channel_id=1, source_target_pairs={{0,8},{1,17},{2,10},{3,19},{4,12},{5,21},{6,14},{7,23},{8,0},{9,25... | collective-permute-start | bytes 884744 | tf_op jit(solution)/shard_map/ppermute | solution.py:37
  193.0 9.4 %collective-permute-start.32 = (bf16[2,112,768]{2,1,0:T(8,128)(2,1)S(1)}, bf16[2,112,768]{2,1,0:T(8,128)(2,1)S(1)}, u32[]{:S(2)}, u32[]{:S(2)}) collective-permute-start(bf16[2,112,768]{2,1,0:T(8,128)(2,1)S(1)} %pad_maximum_fusion.11), channel_id=1, source_target_pairs={{0,4},{1,3},{2,6},{3,1},{4,0},{5,7},{6,2},{7,5},{8,12},{9,11},{10,... | collective-permute-start | bytes 1032200 | tf_op jit(solution)/shard_map/ppermute | solution.py:37
  202.7 5.5 %collective-permute-start.33 = (bf16[1,112,768]{2,1,0:T(8,128)(2,1)S(1)}, bf16[1,112,768]{2,1,0:T(8,128)(2,1)S(1)}, u32[]{:S(2)}, u32[]{:S(2)}) collective-permute-start(bf16[1,112,768]{2,1,0:T(8,128)(2,1)S(1)} %pad_maximum_fusion.14), channel_id=1, source_target_pairs={{0,8},{1,17},{2,10},{3,19},{4,12},{5,21},{6,14},{7,23},{8,0},{9,25... | collective-permute-start | bytes 516104 | tf_op jit(solution)/shard_map/ppermute | solution.py:37
  (7 other events, 26.4 us)
where the time goes:
time: 214 us; the launch traced here: 211 us
  waiting for transfers between devices  99.8 us (47%)
  Pallas kernels  61.8 us (29%)
  starting transfers between devices  28.3 us (13%)
  local copies, waits for them, and re-layouts  10.6 us (5%)
  other arithmetic  8.91 us (4%)
    ppermute x35, waiting for transfers between devices, swap(): return lax.ppermute(array, AXES, list(enumerate(step)))  99.8 us
    pallas_call x9, Pallas kernels, call(): pl.pallas_call(kernel, in_specs=[smem] * len(scalars) + [whole] * len(inp...  61.8 us
    ppermute x35, starting transfers between devices, swap(): return lax.ppermute(array, AXES, list(enumerate(step)))  28.3 us
  transfers between devices with their start and end apart: 35, of which 17 were waited for; matrix products, arithmetic and copies ran while one was open for 5% of the time, Pallas kernels for 26%

commit v1 on v0

--- a/solution.py
+++ b/solution.py
@@ -427,6 +427,16 @@
         side = jnp.concatenate([high, low], axis=0)
         for cut in range(CUTS):
             out_ref[slot_ref[half * out_ref.shape[0] + i * CUTS + cut], main:, :] = side
+
+
+def unpack_kernel(keep_ref, moved_ref, query_ref, key_ref, value_ref, out_ref, side_ref):
+    total = keep_ref[0].astype(F32) + moved_ref[0].astype(F32)
+    rows, cols = query_ref.shape
+    extra = side_ref.shape[0]
+    for i, ref in enumerate((query_ref, key_ref, value_ref)):
+        ref[...] = total[:rows, i * cols : (i + 1) * cols]
+    out_ref[...] = total[:rows, 3 * cols :].T
+    side_ref[...] = total[rows : rows + extra] + total[rows + extra :]
 
 
 def call(kernel, pieces, scalars, inputs, outs, scratch, flops, limit=16):
@@ -639,22 +649,29 @@
     )
     attn_sum = outgoing(attn_keep, attn_send, 8)
     if direct:
-        attn_sum.step(*down_sum.moved, *up_sum.moved)
+        attn_sum.start(*down_sum.moved, *up_sum.moved)
         down_sum.end()
         up_sum.end()
-        attn_sum.start()
+        keep, moved = attn_sum.keep, attn_sum.moved
+        part = keep.shape[0] // 4
+        last = swap(attn_sum.add(keep[3 * part :], moved[1][part:]).astype(BF16), steps[3])
         up_sum.start()
-        both(attn_sum, up_sum)
+        third = attn_sum.add(keep[2 * part : 3 * part], moved[1][:part]).astype(BF16)
+        third = swap(after(third, last), steps[3])
+        second = attn_sum.add(keep[part : 2 * part], moved[0][part:]).astype(BF16)
+        attn_sum.moved = [swap(attn_sum.add(second, last).astype(BF16), steps[2])]
+        first = attn_sum.add(keep[:part], moved[0][:part]).astype(BF16)
+        attn_sum.keep, attn_sum.at = attn_sum.add(first, third).astype(BF16), 2
+        up_sum.hold(last)
+        up_sum.end()
         pair = Sum.merge(down_sum, up_sum)
-        attn_sum.start()
-        pair.start()
+        pair.start(third)
         both(attn_sum, pair)
         attn_sum.start()
         pair.start()
         attn_sum.end()
         finals = [[part] for part in pair.end()[0]]
         attn_sum.start()
-        finals.append(attn_sum.end())
     else:
         side = jnp.concatenate([side_first, side_second], axis=0)
         finals = []
@@ -664,19 +681,25 @@
             package.start()
             finals.append(package.end())
     if direct:
-        attn_grad, side = finals[2][0][0], finals[2][1][0]
+        small = ((rows, cols), F32)
+        query_grad, key_grad, value_grad, out_grad, side = call(
+            unpack_kernel, [], (), (attn_sum.keep, *attn_sum.moved),
+            [small, small, small, ((cols, rows), F32), ((8, width), F32)], [], 1,
+        )
     else:
         attn_grad = finals[2][0]
+        query_grad, key_grad, value_grad = (attn_grad[:, i * cols : (i + 1) * cols] for i in range(3))
+        out_grad = attn_grad[:, 3 * cols :].T
         side = lax.dynamic_index_in_dim(lax.psum(side, AXES), place, keepdims=False)
     return (
         layer_output,
         input_grad,
-        attn_grad[:, :cols],
-        attn_grad[:, cols : 2 * cols],
-        attn_grad[:, 2 * cols : 3 * cols],
+        query_grad,
+        key_grad,
+        value_grad,
         side[7, :cols],
         side[7, 2 * cols : 3 * cols],
-        attn_grad[:, 3 * cols :].T,
+        out_grad,
         side[3],
         side[4],
         side[5],

time: 214 us -> 205 us (0.958)
  waiting for transfers between devices: 99.8 us -> 90.3 us
    ppermute x35 -> x36, waiting for transfers between devices: 99.8 us -> 90.3 us  [swap(): return lax.ppermute(array, AXES, list(enumerate(step)))]
    ppermute x35 -> x36, starting transfers between devices: 28.3 us -> 30.3 us  [swap(): return lax.ppermute(array, AXES, list(enumerate(step)))]
    pallas_call x9 -> x10, Pallas kernels: 61.8 us -> 62.6 us  [call(): pl.pallas_call(kernel, in_specs=[smem] * len(scalars) + [whole] * len(inp...]
  transfers between devices with their start and end apart: 35 -> 36, of which waited for: 17 -> 18; matrix products, arithmetic and copies ran while one was open for 5% -> 6% of each run, Pallas kernels for 26% -> 27%
where the time goes in v1:
time: 205 us; the launch traced here: 203 us
  waiting for transfers between devices  90.3 us (44%)
  Pallas kernels  62.6 us (31%)
  starting transfers between devices  30.3 us (15%)
  local copies, waits for them, and re-layouts  9.09 us (4%)
  other arithmetic  8.6 us (4%)
  between operations  2.05 us (1%)
    ppermute x36, waiting for transfers between devices, swap(): return lax.ppermute(array, AXES, list(enumerate(step)))  90.3 us
    pallas_call x10, Pallas kernels, call(): pl.pallas_call(kernel, in_specs=[smem] * len(scalars) + [whole] * len(inp...  62.6 us
    ppermute x36, starting transfers between devices, swap(): return lax.ppermute(array, AXES, list(enumerate(step)))  30.3 us
  transfers between devices with their start and end apart: 36, of which 18 were waited for; matrix products, arithmetic and copies ran while one was open for 6% of the time, Pallas kernels for 27%

profile of v1, /device:TPU:0, one launch (start us, length us, event | category | flops | bytes accessed | tf_op | source)
XLA Modules:
  0.0 203.0 jit_solution(11819847696722379792)
XLA Ops:
  0.7 0.9 copy.39
  1.5 1.0 maximum_bitcast_fusion.1
  2.5 3.1 %collective-permute-start = (bf16[1,96,768]{2,1,0:T(8,128)(2,1)S(1)}, bf16[1,96,768]{2,1,0:T(8,128)(2,1)S(1)}, u32[]{:S(2)}, u32[]{:S(2)}) collective-permute-start(bf16[1,96,768]{2,1,0:T(8,128)(2,1)S(1)} %maximum_bitcast_fusion.1), channel_id=1, source_target_pairs={{0,8},{1,17},{2,10},{3,19},{4,12},{5,21},{6,14},{7,23},{8,0},{9,25... | collective-permute-start | bytes 442376 | tf_op jit(solution)/shard_map/ppermute | solution.py:37
  5.6 0.8 reshape.149
  6.4 0.8 reshape.150
  7.2 1.0 maximum_bitcast_fusion
  8.2 1.7 collective-permute-done
  9.9 2.3 %collective-permute-start.2 = (bf16[1,2,96,768]{3,2,0,1:T(8,128)(2,1)S(1)}, bf16[1,2,96,768]{3,2,0,1:T(8,128)(2,1)S(1)}, u32[]{:S(2)}, u32[]{:S(2)}) collective-permute-start(bf16[1,2,96,768]{3,2,0,1:T(8,128)(2,1)S(1)} %maximum_bitcast_fusion), channel_id=1, source_target_pairs={{0,8},{1,17},{2,10},{3,19},{4,12},{5,21},{6,14},{7,23},{8,0},{9,25... | collective-permute-start | bytes 884744 | tf_op jit(solution)/shard_map/ppermute | solution.py:37
  12.2 0.8 dynamic_slice.17
  13.0 1.6 collective-permute-start.1
  14.6 5.4 %collective-permute-done.2 = bf16[1,2,96,768]{3,2,0,1:T(8,128)(2,1)S(1)} collective-permute-done((bf16[1,2,96,768]{3,2,0,1:T(8,128)(2,1)S(1)}, bf16[1,2,96,768]{3,2,0,1:T(8,128)(2,1)S(1)}, u32[]{:S(2)}, u32[]{:S(2)}) %collective-permute-start.2) | collective-permute-done | bytes 294944 | tf_op jit(solution)/shard_map/ppermute | solution.py:37
  20.1 2.4 %collective-permute-start.3 = (bf16[4,96,768]{2,1,0:T(8,128)(2,1)S(1)}, bf16[4,96,768]{2,1,0:T(8,128)(2,1)S(1)}, u32[]{:S(2)}, u32[]{:S(2)}) collective-permute-start(bf16[4,96,768]{2,1,0:T(8,128)(2,1)S(1)} %pad_maximum_fusion.7), channel_id=1, source_target_pairs={{0,16},{1,9},{2,18},{3,11},{4,20},{5,13},{6,22},{7,15},{8,24},{9,1... | collective-permute-start | bytes 1769480 | tf_op jit(solution)/shard_map/ppermute | solution.py:37
  22.5 1.5 collective-permute-start.4
  24.0 13.3 %collective-permute-done.3 = bf16[4,96,768]{2,1,0:T(8,128)(2,1)S(1)} collective-permute-done((bf16[4,96,768]{2,1,0:T(8,128)(2,1)S(1)}, bf16[4,96,768]{2,1,0:T(8,128)(2,1)S(1)}, u32[]{:S(2)}, u32[]{:S(2)}) %collective-permute-start.3) | collective-permute-done | bytes 589856 | tf_op jit(solution)/shard_map/ppermute | solution.py:37
  37.5 1.8 collective-permute-start.5
  39.3 0.9 slice_bitcast_fusion
  40.3 17.1 %collective-permute-done.6 = bf16[4,96,768]{2,1,0:T(8,128)(2,1)S(1)} collective-permute-done((bf16[4,96,768]{2,1,0:T(8,128)(2,1)S(1)}, bf16[4,96,768]{2,1,0:T(8,128)(2,1)S(1)}, u32[]{:S(2)}, u32[]{:S(2)}) %collective-permute-start.6) | collective-permute-done | bytes 589856 | tf_op jit(solution)/shard_map/ppermute | solution.py:37
  60.0 1.7 collective-permute-start.13
  61.7 7.6 %shard_map.332 = (bf16[2,768,768]{2,1,0:T(8,128)(2,1)S(1)}, bf16[2,512,576]{2,1,0:T(8,128)(2,1)S(1)}, bf16[2,192,512]{2,1,0:T(8,128)(2,1)S(1)}, bf16[2,3,512,512...) custom-call(s32[32]{0:T(128)S(1)} %fusion.35.place_ref, ...), custom_call_target="tpu_custom_call" | custom-call | flops 1024 | bytes 1024 | tf_op jit(solution)/shard_map/pallas_call | solution.py:445
  69.4 8.7 %shard_map.333 = (bf16[2,768,768]{2,1,0:T(8,128)(2,1)S(1)}, bf16[2,512,576]{2,1,0:T(8,128)(2,1)S(1)}, bf16[2,192,512]{2,1,0:T(8,128)(2,1)S(1)}, bf16[2,3,512,512...) custom-call(s32[32]{0:T(128)S(1)} %fusion.35.place_ref, ...), custom_call_target="tpu_custom_call" | custom-call | flops 1024 | bytes 1024 | tf_op jit(solution)/shard_map/pallas_call | solution.py:445
  78.7 1.9 collective-permute-done.13.rest_2_
  80.9 1.0 collective-permute-done.10.rest_2_
  82.0 1.0 collective-permute-done.11.rest_3_
  83.0 6.9 %shard_map.334 = (bf16[2,768,768]{2,1,0:T(8,128)(2,1)S(1)}, bf16[2,512,768]{2,1,0:T(8,128)(2,1)S(1)}, bf16[2,512,768]{2,1,0:T(8,128)(2,1)S(1)}, bf16[2,768,768]{...) custom-call(s32[32]{0:T(128)S(1)} %fusion.35.place_ref, ...), custom_call_target="tpu_custom_call" | custom-call | flops 1024 | bytes 1024 | tf_op jit(solution)/shard_map/pallas_call | solution.py:445
  92.2 2.7 %shard_map.335 = (bf16[2,768,768]{2,1,0:T(8,128)(2,1)S(1)}, f32[512,768]{1,0:T(8,128)S(1)}) custom-call(s32[32]{0:T(128)S(1)} %fusion.35.place_ref, bf16[2,512,768]{2,1,0:T(8,128)(2,1)S(1)} %get-tuple-element.107.active_ref, f32[512,768]{1,0:T(8,128)S(1)} %get-tuple-element.108.normal_ref.rest_2_, f32[1,768]{1,0:T(1,128)S(1)} %stack.50.rest_1_.first_gain.rest_4_, ...), custom_call_target="tpu_custom_call" | custom-call | flops 1024 | bytes 1024 | tf_op jit(solution)/shard_map/pallas_call | solution.py:445
  95.0 6.2 %shard_map.336 = (bf16[2,768,768]{2,1,0:T(8,128)(2,1)S(1)}, f32[512,768]{1,0:T(8,128)}, f32[512,768]{1,0:T(8,128)S(1)}, bf16[512,768]{1,0:T(8,128)(2,1)S(1)}, bf...) custom-call(s32[32]{0:T(128)S(1)} %fusion.35.place_ref, ...), custom_call_target="tpu_custom_call" | custom-call | flops 1024 | bytes 1024 | tf_op jit(solution)/shard_map/pallas_call | solution.py:445
  102.0 2.1 %shard_map.337 = bf16[16,96,768]{2,1,0:T(8,128)(2,1)S(1)} custom-call(s32[32]{0:T(128)S(1)} %fusion.36.slot_ref, bf16[2,512,768]{2,1,0:T(8,128)(2,1)S(1)} %get-tuple-element.107.active_ref, bf16[768,512]{1,0:T(8,128)(2,1)S(1)} %get-tuple-element.120.turned_ref), custom_call_target="tpu_custom_call" | custom-call | flops 1024 | bytes 1024 | tf_op jit(solution)/shard_map/pallas_call | solution.py:445
  104.3 1.7 collective-permute-done.19
  107.1 5.0 %shard_map.338 = (bf16[16,96,768]{2,1,0:T(8,128)(2,1)S(1)}, f32[8,768]{1,0:T(8,128)S(1)}, f32[512,768]{1,0:T(8,128)S(1)}, bf16[768,512]{1,0:T(8,128)(2,1)S(1)}) custom-call(s32[32]{0:T(128)S(1)} %fusion.36.slot_ref, bf16[512,768]{1,0:T(8,128)(2,1)S(1)} %get-tuple-element.122.low_grad_ref, bf16[2,512,768]{2,1,0:T(8,128)(2,1)S(1)} %get-tuple-element.112.slope_ref, ...), custom_call_target="tpu_custom_call" | custom-call | flops 1024 | bytes 1024 | tf_op jit(solution)/shard_map/pallas_call | solution.py:445
  112.3 1.1 collective-permute-start.21
  113.4 5.8 %shard_map.339 = (bf16[16,96,768]{2,1,0:T(8,128)(2,1)S(1)}, f32[8,768]{1,0:T(8,128)S(1)}, f32[512,768]{1,0:T(8,128)S(1)}, bf16[512,768]{1,0:T(8,128)(2,1)S(1)}, bf16[768,512]{1,0:T(8,128)(2,1)S(1)}) custom-call(s32[32]{0:T(128)S(1)} %fusion.36.slot_ref, bf16[512,768]{1,0:T(8,128)(2,1)S(1)} %get-tuple-element.122.low_grad_ref, ...), custom_call_target="tpu_custom_call" | custom-call | flops 1024 | bytes 1024 | tf_op jit(solution)/shard_map/pallas_call | solution.py:445
  119.2 3.8 %collective-permute-done.23 = bf16[8,96,768]{2,1,0:T(8,128)(2,1)S(1)} collective-permute-done((bf16[8,96,768]{2,1,0:T(8,128)(2,1)S(1)}, bf16[8,96,768]{2,1,0:T(8,128)(2,1)S(1)}, u32[]{:S(2)}, u32[]{:S(2)}) %collective-permute-start.23) | collective-permute-done | bytes 1179680 | tf_op jit(solution)/shard_map/ppermute | solution.py:37
  123.4 0.7 add_convert_fusion
  124.5 2.4 %collective-permute-start.24 = (bf16[4,96,768]{2,1,0:T(8,128)(2,1)S(1)}, bf16[4,96,768]{2,1,0:T(8,128)(2,1)S(1)}, u32[]{:S(2)}, u32[]{:S(2)}) collective-permute-start(bf16[4,96,768]{2,1,0:T(8,128)(2,1)S(1)} %get-tuple-element.154), channel_id=1, source_target_pairs={{0,16},{1,9},{2,18},{3,11},{4,20},{5,13},{6,22},{7,15},{8,24},{9,1... | collective-permute-start | bytes 1769480 | tf_op jit(solution)/shard_map/ppermute | solution.py:37
  127.0 16.8 %shard_map.340 = (f32[512,768]{1,0:T(8,128)}, f32[2,8,768]{2,1,0:T(8,128)}, f32[2,8,768]{2,1,0:T(8,128)}, bf16[16,112,768]{2,1,0:T(8,128)(2,1)S(1)}, bf16[16,112,768]{2,1,0:T(8,128)(2,1)S(1)}) custom-call(s32[32]{0:T(128)S(1)} %fusion.36.slot_ref, bf16[768,512]{1,0:T(8,128)(2,1)S(1)} %get-tuple-element.118.turned_ref, ...), custom_call_target="tpu_custom_call" | custom-call | flops 1024 | bytes 1024 | tf_op jit(solution)/shard_map/pallas_call | solution.py:445
  146.2 1.1 collective-permute-done.26
  147.7 1.6 collective-permute-done.27
  150.2 1.8 collective-permute-start.28
  152.3 10.4 %collective-permute-done.31 = bf16[4,96,768]{2,1,0:T(8,128)(2,1)S(1)} collective-permute-done((bf16[4,96,768]{2,1,0:T(8,128)(2,1)S(1)}, bf16[4,96,768]{2,1,0:T(8,128)(2,1)S(1)}, u32[]{:S(2)}, u32[]{:S(2)}) %collective-permute-start.31) | collective-permute-done | bytes 589856 | tf_op jit(solution)/shard_map/ppermute | solution.py:37
  162.7 1.7 collective-permute-start.29
  165.2 8.8 %collective-permute-done.29 = bf16[4,112,768]{2,1,0:T(8,128)(2,1)S(1)} collective-permute-done((bf16[4,112,768]{2,1,0:T(8,128)(2,1)S(1)}, bf16[4,112,768]{2,1,0:T(8,128)(2,1)S(1)}, u32[]{:S(2)}, u32[]{:S(2)}) %collective-permute-start.29) | collective-permute-done | bytes 688160 | tf_op jit(solution)/shard_map/ppermute | solution.py:37
  174.0 1.6 collective-permute-start.32
  176.1 10.6 %collective-permute-done.30 = bf16[4,112,768]{2,1,0:T(8,128)(2,1)S(1)} collective-permute-done((bf16[4,112,768]{2,1,0:T(8,128)(2,1)S(1)}, bf16[4,112,768]{2,1,0:T(8,128)(2,1)S(1)}, u32[]{:S(2)}, u32[]{:S(2)}) %collective-permute-start.30) | collective-permute-done | bytes 688160 | tf_op jit(solution)/shard_map/ppermute | solution.py:37
  187.4 6.5 %collective-permute-done.35 = bf16[1,2,96,768]{3,2,0,1:T(8,128)(2,1)S(1)} collective-permute-done((bf16[1,2,96,768]{3,2,0,1:T(8,128)(2,1)S(1)}, bf16[1,2,96,768]{3,2,0,1:T(8,128)(2,1)S(1)}, u32[]{:S(2)}, u32[]{:S(2)}) %collective-permute-start.35) | collective-permute-done | bytes 294944 | tf_op jit(solution)/shard_map/ppermute | solution.py:37
  194.0 0.8 slice_bitcast_fusion.2
  195.0 1.8 collective-permute-start.34
  196.8 3.7 %collective-permute-done.34.moved_ref = bf16[1,112,768]{2,1,0:T(8,128)(2,1)S(1)} collective-permute-done((bf16[1,112,768]{2,1,0:T(8,128)(2,1)S(1)}, bf16[1,112,768]{2,1,0:T(8,128)(2,1)S(1)}, u32[]{:S(2)}, u32[]{:S(2)}) %collective-permute-start.34) | collective-permute-done | bytes 172064 | tf_op jit(solution)/shard_map/ppermute | solution.py:37
  200.5 0.8 shard_map.341
  (170 shorter events, 16.8 us)
Async XLA Ops:
  2.5 7.4 %collective-permute-start = (bf16[1,96,768]{2,1,0:T(8,128)(2,1)S(1)}, bf16[1,96,768]{2,1,0:T(8,128)(2,1)S(1)}, u32[]{:S(2)}, u32[]{:S(2)}) collective-permute-start(bf16[1,96,768]{2,1,0:T(8,128)(2,1)S(1)} %maximum_bitcast_fusion.1), channel_id=1, source_target_pairs={{0,8},{1,17},{2,10},{3,19},{4,12},{5,21},{6,14},{7,23},{8,0},{9,25... | collective-permute-start | bytes 442376 | tf_op jit(solution)/shard_map/ppermute | solution.py:37
  9.9 10.0 %collective-permute-start.2 = (bf16[1,2,96,768]{3,2,0,1:T(8,128)(2,1)S(1)}, bf16[1,2,96,768]{3,2,0,1:T(8,128)(2,1)S(1)}, u32[]{:S(2)}, u32[]{:S(2)}) collective-permute-start(bf16[1,2,96,768]{3,2,0,1:T(8,128)(2,1)S(1)} %maximum_bitcast_fusion), channel_id=1, source_target_pairs={{0,8},{1,17},{2,10},{3,19},{4,12},{5,21},{6,14},{7,23},{8,0},{9,25... | collective-permute-start | bytes 884744 | tf_op jit(solution)/shard_map/ppermute | solution.py:37
  13.0 7.0 %collective-permute-start.1 = (bf16[2,96,768]{2,1,0:T(8,128)(2,1)S(1)}, bf16[2,96,768]{2,1,0:T(8,128)(2,1)S(1)}, u32[]{:S(2)}, u32[]{:S(2)}) collective-permute-start(bf16[2,96,768]{2,1,0:T(8,128)(2,1)S(1)} %pad_maximum_fusion.13), channel_id=1, source_target_pairs={{0,4},{1,3},{2,6},{3,1},{4,0},{5,7},{6,2},{7,5},{8,12},{9,11},{10,... | collective-permute-start | bytes 884744 | tf_op jit(solution)/shard_map/ppermute | solution.py:37
  20.1 17.2 %collective-permute-start.3 = (bf16[4,96,768]{2,1,0:T(8,128)(2,1)S(1)}, bf16[4,96,768]{2,1,0:T(8,128)(2,1)S(1)}, u32[]{:S(2)}, u32[]{:S(2)}) collective-permute-start(bf16[4,96,768]{2,1,0:T(8,128)(2,1)S(1)} %pad_maximum_fusion.7), channel_id=1, source_target_pairs={{0,16},{1,9},{2,18},{3,11},{4,20},{5,13},{6,22},{7,15},{8,24},{9,1... | collective-permute-start | bytes 1769480 | tf_op jit(solution)/shard_map/ppermute | solution.py:37
  22.5 14.9 %collective-permute-start.4 = (bf16[2,2,96,768]{3,2,0,1:T(8,128)(2,1)S(1)}, bf16[2,2,96,768]{3,2,0,1:T(8,128)(2,1)S(1)}, u32[]{:S(2)}, u32[]{:S(2)}) collective-permute-start(bf16[2,2,96,768]{3,2,0,1:T(8,128)(2,1)S(1)} %pad_maximum_fusion.8), channel_id=1, source_target_pairs={{0,4},{1,3},{2,6},{3,1},{4,0},{5,7},{6,2},{7,5},{8,12},{9,11},{10,... | collective-permute-start | bytes 1769480 | tf_op jit(solution)/shard_map/ppermute | solution.py:37
  37.5 19.9 %collective-permute-start.5 = (bf16[8,96,768]{2,1,0:T(8,128)(2,1)S(1)}, bf16[8,96,768]{2,1,0:T(8,128)(2,1)}, u32[]{:S(2)}, u32[]{:S(2)}) collective-permute-start(bf16[8,96,768]{2,1,0:T(8,128)(2,1)S(1)} %pad_maximum_fusion.rest_1_), channel_id=1, source_target_pairs={{0,2},{1,5},{2,0},{3,7},{4,6},{5,1},{6,4},{7,3},{8,10},{9,13},{10,... | collective-permute-start | bytes 3538952 | tf_op jit(solution)/shard_map/ppermute | solution.py:37
  40.2 18.4 %copy-start.14 = (f32[768]{0:T(1024)S(1)}, f32[768]{0:T(1024)}, u32[]{:S(2)}) copy-start(f32[768]{0:T(1024)} %param.30) | copy-start | bytes 9220
  40.2 18.4 %copy-start.15 = (f32[768]{0:T(1024)S(1)}, f32[768]{0:T(1024)}, u32[]{:S(2)}) copy-start(f32[768]{0:T(1024)} %param.31) | copy-start | bytes 9220
  40.2 18.4 %copy-start.16 = (f32[768]{0:T(1024)S(1)}, f32[768]{0:T(1024)}, u32[]{:S(2)}) copy-start(f32[768]{0:T(1024)} %param.29) | copy-start | bytes 9220
  40.2 21.5 %copy-start = (bf16[512,768]{1,0:T(8,128)(2,1)S(1)}, bf16[512,768]{1,0:T(8,128)(2,1)}, u32[]{:S(2)}) copy-start(bf16[512,768]{1,0:T(8,128)(2,1)} %tokens_ref.3) | copy-start | bytes 2359300
  40.2 17.2 %collective-permute-start.6 = (bf16[4,96,768]{2,1,0:T(8,128)(2,1)S(1)}, bf16[4,96,768]{2,1,0:T(8,128)(2,1)S(1)}, u32[]{:S(2)}, u32[]{:S(2)}) collective-permute-start(bf16[4,96,768]{2,1,0:T(8,128)(2,1)S(1)} %get-tuple-element.221), channel_id=1, source_target_pairs={{0,16},{1,9},{2,18},{3,11},{4,20},{5,13},{6,22},{7,15},{8,24},{9,1... | collective-permute-start | bytes 1769480 | tf_op jit(solution)/shard_map/ppermute | solution.py:37
  57.5 11.9 %collective-permute-start.7 = (bf16[8,96,768]{2,1,0:T(8,128)(2,1)S(1)}, bf16[8,96,768]{2,1,0:T(8,128)(2,1)}, u32[]{:S(2)}, u32[]{:S(2)}) collective-permute-start(bf16[8,96,768]{2,1,0:T(8,128)(2,1)S(1)} %pad_maximum_fusion.rest_1_), channel_id=1, source_target_pairs={{0,1},{1,0},{2,3},{3,2},{4,5},{5,4},{6,7},{7,6},{8,9},{9,8},{10,11... | collective-permute-start | bytes 3538952 | tf_op jit(solution)/shard_map/ppermute | solution.py:37
  57.6 11.8 %collective-permute-start.8 = (bf16[8,96,768]{2,1,0:T(8,128)(2,1)}, bf16[8,96,768]{2,1,0:T(8,128)(2,1)}, u32[]{:S(2)}, u32[]{:S(2)}) collective-permute-start(bf16[8,96,768]{2,1,0:T(8,128)(2,1)} %collective-permute-done.5.rest_2_), channel_id=1, source_target_pairs={{0,1},{1,0},{2,3},{3,2},{4,5},{5,4},{6,7},{7,6},{8,9},{9,8},{10,11... | collective-permute-start | bytes 3538952 | tf_op jit(solution)/shard_map/ppermute | solution.py:37
  58.1 20.1 %collective-permute-start.9 = (bf16[8,96,768]{2,1,0:T(8,128)(2,1)S(1)}, bf16[8,96,768]{2,1,0:T(8,128)(2,1)}, u32[]{:S(2)}, u32[]{:S(2)}) collective-permute-start(bf16[8,96,768]{2,1,0:T(8,128)(2,1)S(1)} %pad_maximum_fusion.2.rest_0_), channel_id=1, source_target_pairs={{0,2},{1,5},{2,0},{3,7},{4,6},{5,1},{6,4},{7,3},{8,10},{9,13},{10,... | collective-permute-start | bytes 3538952 | tf_op jit(solution)/shard_map/ppermute | solution.py:37
  60.0 20.6 %collective-permute-start.13 = (bf16[4,96,768]{2,1,0:T(8,128)(2,1)}, bf16[4,96,768]{2,1,0:T(8,128)(2,1)S(1)}, u32[]{:S(2)}, u32[]{:S(2)}) collective-permute-start(bf16[4,96,768]{2,1,0:T(8,128)(2,1)} %get-tuple-element.113.rest_0_), channel_id=1, source_target_pairs={{0,2},{1,5},{2,0},{3,7},{4,6},{5,1},{6,4},{7,3},{8,10},{9,13},{10,... | collective-permute-start | bytes 1769480 | tf_op jit(solution)/shard_map/ppermute | solution.py:37
  61.7 18.9 %collective-permute-start.12 = (bf16[4,96,768]{2,1,0:T(8,128)(2,1)}, bf16[4,96,768]{2,1,0:T(8,128)(2,1)S(1)}, u32[]{:S(2)}, u32[]{:S(2)}) collective-permute-start(bf16[4,96,768]{2,1,0:T(8,128)(2,1)} %get-tuple-element.113.rest_0_), channel_id=1, source_target_pairs={{0,16},{1,9},{2,18},{3,11},{4,20},{5,13},{6,22},{7,15},{8,24},{9,1... | collective-permute-start | bytes 1769480 | tf_op jit(solution)/shard_map/ppermute | solution.py:37
  69.4 8.7 %copy-start.2 = (bf16[2,512,576]{2,1,0:T(8,128)(2,1)}, bf16[2,512,576]{2,1,0:T(8,128)(2,1)S(1)}, u32[]{:S(2)}) copy-start(bf16[2,512,576]{2,1,0:T(8,128)(2,1)S(1)} %get-tuple-element.146.rest_7_) | copy-start | bytes 3538948
  69.4 8.7 %copy-start.7 = (bf16[2,192,512]{2,1,0:T(8,128)(2,1)}, bf16[2,192,512]{2,1,0:T(8,128)(2,1)S(1)}, u32[]{:S(2)}) copy-start(bf16[2,192,512]{2,1,0:T(8,128)(2,1)S(1)} %get-tuple-element.147.rest_8_) | copy-start | bytes 1179652
  69.4 13.6 %copy-start.13 = (f32[3072]{0:T(1024)S(1)}, f32[3072]{0:T(1024)}, u32[]{:S(2)}) copy-start(f32[3072]{0:T(1024)} %param.33) | copy-start | bytes 36868
  78.1 11.8 %copy-start.4 = (bf16[2,512,576]{2,1,0:T(8,128)(2,1)}, bf16[2,512,576]{2,1,0:T(8,128)(2,1)S(1)}, u32[]{:S(2)}) copy-start(bf16[2,512,576]{2,1,0:T(8,128)(2,1)S(1)} %get-tuple-element.141.rest_1_) | copy-start | bytes 3538948
  78.1 11.8 %copy-start.9 = (bf16[2,192,512]{2,1,0:T(8,128)(2,1)}, bf16[2,192,512]{2,1,0:T(8,128)(2,1)S(1)}, u32[]{:S(2)}) copy-start(bf16[2,192,512]{2,1,0:T(8,128)(2,1)S(1)} %get-tuple-element.142.rest_2_) | copy-start | bytes 1179652
  78.1 11.8 %copy-start.11 = (f32[512,1]{1,0:T(8,128)}, f32[512,1]{1,0:T(8,128)S(1)}, u32[]{:S(2)}) copy-start(f32[512,1]{1,0:T(8,128)S(1)} %get-tuple-element.103.rest_3_) | copy-start | bytes 6148
  78.1 3.8 %collective-permute-start.10 = (bf16[8,96,768]{2,1,0:T(8,128)(2,1)S(1)}, bf16[8,96,768]{2,1,0:T(8,128)(2,1)S(1)}, u32[]{:S(2)}, u32[]{:S(2)}) collective-permute-start(bf16[8,96,768]{2,1,0:T(8,128)(2,1)S(1)} %pad_maximum_fusion.2.rest_0_), channel_id=1, source_target_pairs={{0,1},{1,0},{2,3},{3,2},{4,5},{5,4},{6,7},{7,6},{8,9},{9,8},{10,11... | collective-permute-start | bytes 3538952 | tf_op jit(solution)/shard_map/ppermute | solution.py:37
  78.2 4.7 %collective-permute-start.11 = (bf16[8,96,768]{2,1,0:T(8,128)(2,1)}, bf16[8,96,768]{2,1,0:T(8,128)(2,1)S(1)}, u32[]{:S(2)}, u32[]{:S(2)}) collective-permute-start(bf16[8,96,768]{2,1,0:T(8,128)(2,1)} %collective-permute-done.9.rest_1_), channel_id=1, source_target_pairs={{0,1},{1,0},{2,3},{3,2},{4,5},{5,4},{6,7},{7,6},{8,9},{9,8},{10,11... | collective-permute-start | bytes 3538952 | tf_op jit(solution)/shard_map/ppermute | solution.py:37
  80.6 9.9 %collective-permute-start.14 = (bf16[4,96,768]{2,1,0:T(8,128)(2,1)S(1)}, bf16[4,96,768]{2,1,0:T(8,128)(2,1)S(1)}, u32[]{:S(2)}, u32[]{:S(2)}) collective-permute-start(bf16[4,96,768]{2,1,0:T(8,128)(2,1)S(1)} %collective-permute-done.12.rest_1_), channel_id=1, source_target_pairs={{0,2},{1,5},{2,0},{3,7},{4,6},{5,1},{6,4},{7,3},{8,10},{9,13},{10,... | collective-permute-start | bytes 1769480 | tf_op jit(solution)/shard_map/ppermute | solution.py:37
  83.0 8.5 %copy-start.18 = (f32[768]{0:T(1024)S(1)}, f32[768]{0:T(1024)}, u32[]{:S(2)}) copy-start(f32[768]{0:T(1024)} %param.36) | copy-start | bytes 9220
  83.0 8.6 %copy-start.19 = (f32[768]{0:T(1024)S(1)}, f32[768]{0:T(1024)}, u32[]{:S(2)}) copy-start(f32[768]{0:T(1024)} %param.37) | copy-start | bytes 9220
  90.5 4.5 %collective-permute-start.15 = (bf16[4,96,768]{2,1,0:T(8,128)(2,1)S(1)}, bf16[4,96,768]{2,1,0:T(8,128)(2,1)S(1)}, u32[]{:S(2)}, u32[]{:S(2)}) collective-permute-start(bf16[4,96,768]{2,1,0:T(8,128)(2,1)S(1)} %copy-done.1), channel_id=1, source_target_pairs={{0,1},{1,0},{2,3},{3,2},{4,5},{5,4},{6,7},{7,6},{8,9},{9,8},{10,11... | collective-permute-start | bytes 1769480 | tf_op jit(solution)/shard_map/ppermute | solution.py:37
  90.5 4.5 %collective-permute-start.16 = (bf16[4,96,768]{2,1,0:T(8,128)(2,1)S(1)}, bf16[4,96,768]{2,1,0:T(8,128)(2,1)S(1)}, u32[]{:S(2)}, u32[]{:S(2)}) collective-permute-start(bf16[4,96,768]{2,1,0:T(8,128)(2,1)S(1)} %collective-permute-done.12.rest_1_), channel_id=1, source_target_pairs={{0,1},{1,0},{2,3},{3,2},{4,5},{5,4},{6,7},{7,6},{8,9},{9,8},{10,11... | collective-permute-start | bytes 1769480 | tf_op jit(solution)/shard_map/ppermute | solution.py:37
  91.0 4.0 %collective-permute-start.17 = (bf16[4,96,768]{2,1,0:T(8,128)(2,1)S(1)}, bf16[4,96,768]{2,1,0:T(8,128)(2,1)S(1)}, u32[]{:S(2)}, u32[]{:S(2)}) collective-permute-start(bf16[4,96,768]{2,1,0:T(8,128)(2,1)S(1)} %collective-permute-done.13.rest_2_), channel_id=1, source_target_pairs={{0,1},{1,0},{2,3},{3,2},{4,5},{5,4},{6,7},{7,6},{8,9},{9,8},{10,11... | collective-permute-start | bytes 1769480 | tf_op jit(solution)/shard_map/ppermute | solution.py:37
  91.0 4.0 %collective-permute-start.18 = (bf16[4,96,768]{2,1,0:T(8,128)(2,1)S(1)}, bf16[4,96,768]{2,1,0:T(8,128)(2,1)S(1)}, u32[]{:S(2)}, u32[]{:S(2)}) collective-permute-start(bf16[4,96,768]{2,1,0:T(8,128)(2,1)S(1)} %collective-permute-done.14.rest_3_), channel_id=1, source_target_pairs={{0,1},{1,0},{2,3},{3,2},{4,5},{5,4},{6,7},{7,6},{8,9},{9,8},{10,11... | collective-permute-start | bytes 1769480 | tf_op jit(solution)/shard_map/ppermute | solution.py:37
  101.4 2.9 %collective-permute-start.22 = (bf16[8,96,768]{2,1,0:T(8,128)(2,1)S(1)}, bf16[8,96,768]{2,1,0:T(8,128)(2,1)S(1)}, u32[]{:S(2)}, u32[]{:S(2)}) collective-permute-start(bf16[8,96,768]{2,1,0:T(8,128)(2,1)S(1)} %get-tuple-element.208), channel_id=1, source_target_pairs={{0,1},{1,0},{2,3},{3,2},{4,5},{5,4},{6,7},{7,6},{8,9},{9,8},{10,11... | collective-permute-start | bytes 3538952 | tf_op jit(solution)/shard_map/ppermute | solution.py:37
  101.6 4.4 %collective-permute-start.19 = (bf16[8,96,768]{2,1,0:T(8,128)(2,1)S(1)}, bf16[8,96,768]{2,1,0:T(8,128)(2,1)S(1)}, u32[]{:S(2)}, u32[]{:S(2)}) collective-permute-start(bf16[8,96,768]{2,1,0:T(8,128)(2,1)S(1)} %get-tuple-element.209), channel_id=1, source_target_pairs={{0,1},{1,0},{2,3},{3,2},{4,5},{5,4},{6,7},{7,6},{8,9},{9,8},{10,11... | collective-permute-start | bytes 3538952 | tf_op jit(solution)/shard_map/ppermute | solution.py:37
  106.7 16.3 %collective-permute-start.23 = (bf16[8,96,768]{2,1,0:T(8,128)(2,1)S(1)}, bf16[8,96,768]{2,1,0:T(8,128)(2,1)S(1)}, u32[]{:S(2)}, u32[]{:S(2)}) collective-permute-start(bf16[8,96,768]{2,1,0:T(8,128)(2,1)S(1)} %get-tuple-element.207), channel_id=1, source_target_pairs={{0,2},{1,5},{2,0},{3,7},{4,6},{5,1},{6,4},{7,3},{8,10},{9,13},{10,... | collective-permute-start | bytes 3538952 | tf_op jit(solution)/shard_map/ppermute | solution.py:37
  112.3 11.0 %collective-permute-start.21 = (bf16[8,96,768]{2,1,0:T(8,128)(2,1)S(1)}, bf16[8,96,768]{2,1,0:T(8,128)(2,1)S(1)}, u32[]{:S(2)}, u32[]{:S(2)}) collective-permute-start(bf16[8,96,768]{2,1,0:T(8,128)(2,1)S(1)} %get-tuple-element.210), channel_id=1, source_target_pairs={{0,1},{1,0},{2,3},{3,2},{4,5},{5,4},{6,7},{7,6},{8,9},{9,8},{10,11... | collective-permute-start | bytes 3538952 | tf_op jit(solution)/shard_map/ppermute | solution.py:37
  113.4 9.9 %collective-permute-start.20 = (bf16[8,96,768]{2,1,0:T(8,128)(2,1)S(1)}, bf16[8,96,768]{2,1,0:T(8,128)(2,1)S(1)}, u32[]{:S(2)}, u32[]{:S(2)}) collective-permute-start(bf16[8,96,768]{2,1,0:T(8,128)(2,1)S(1)} %get-tuple-element.211), channel_id=1, source_target_pairs={{0,1},{1,0},{2,3},{3,2},{4,5},{5,4},{6,7},{7,6},{8,9},{9,8},{10,11... | collective-permute-start | bytes 3538952 | tf_op jit(solution)/shard_map/ppermute | solution.py:37
  124.1 19.8 %collective-permute-start.25 = (bf16[8,96,768]{2,1,0:T(8,128)(2,1)S(1)}, bf16[8,96,768]{2,1,0:T(8,128)(2,1)S(1)}, u32[]{:S(2)}, u32[]{:S(2)}) collective-permute-start(bf16[8,96,768]{2,1,0:T(8,128)(2,1)S(1)} %get-tuple-element.205), channel_id=1, source_target_pairs={{0,2},{1,5},{2,0},{3,7},{4,6},{5,1},{6,4},{7,3},{8,10},{9,13},{10,... | collective-permute-start | bytes 3538952 | tf_op jit(solution)/shard_map/ppermute | solution.py:37
  124.5 19.4 %collective-permute-start.24 = (bf16[4,96,768]{2,1,0:T(8,128)(2,1)S(1)}, bf16[4,96,768]{2,1,0:T(8,128)(2,1)S(1)}, u32[]{:S(2)}, u32[]{:S(2)}) collective-permute-start(bf16[4,96,768]{2,1,0:T(8,128)(2,1)S(1)} %get-tuple-element.154), channel_id=1, source_target_pairs={{0,16},{1,9},{2,18},{3,11},{4,20},{5,13},{6,22},{7,15},{8,24},{9,1... | collective-permute-start | bytes 1769480 | tf_op jit(solution)/shard_map/ppermute | solution.py:37
  144.1 3.2 %collective-permute-start.26 = (bf16[8,112,768]{2,1,0:T(8,128)(2,1)S(1)}, bf16[8,112,768]{2,1,0:T(8,128)(2,1)S(1)}, u32[]{:S(2)}, u32[]{:S(2)}) collective-permute-start(bf16[8,112,768]{2,1,0:T(8,128)(2,1)S(1)} %get-tuple-element.198), channel_id=1, source_target_pairs={{0,1},{1,0},{2,3},{3,2},{4,5},{5,4},{6,7},{7,6},{8,9},{9,8},{10,11... | collective-permute-start | bytes 4128776 | tf_op jit(solution)/shard_map/ppermute | solution.py:37
  144.1 5.1 %collective-permute-start.27 = (bf16[8,112,768]{2,1,0:T(8,128)(2,1)S(1)}, bf16[8,112,768]{2,1,0:T(8,128)(2,1)S(1)}, u32[]{:S(2)}, u32[]{:S(2)}) collective-permute-start(bf16[8,112,768]{2,1,0:T(8,128)(2,1)S(1)} %get-tuple-element.199), channel_id=1, source_target_pairs={{0,1},{1,0},{2,3},{3,2},{4,5},{5,4},{6,7},{7,6},{8,9},{9,8},{10,11... | collective-permute-start | bytes 4128776 | tf_op jit(solution)/shard_map/ppermute | solution.py:37
  145.5 17.1 %collective-permute-start.31 = (bf16[4,96,768]{2,1,0:T(8,128)(2,1)S(1)}, bf16[4,96,768]{2,1,0:T(8,128)(2,1)S(1)}, u32[]{:S(2)}, u32[]{:S(2)}) collective-permute-start(bf16[4,96,768]{2,1,0:T(8,128)(2,1)S(1)} %get-tuple-element.202), channel_id=1, source_target_pairs={{0,16},{1,9},{2,18},{3,11},{4,20},{5,13},{6,22},{7,15},{8,24},{9,1... | collective-permute-start | bytes 1769480 | tf_op jit(solution)/shard_map/ppermute | solution.py:37
  150.2 12.5 %collective-permute-start.28 = (bf16[4,112,768]{2,1,0:T(8,128)(2,1)S(1)}, bf16[4,112,768]{2,1,0:T(8,128)(2,1)S(1)}, u32[]{:S(2)}, u32[]{:S(2)}) collective-permute-start(bf16[4,112,768]{2,1,0:T(8,128)(2,1)S(1)} %pad_maximum_fusion.4), channel_id=1, source_target_pairs={{0,2},{1,5},{2,0},{3,7},{4,6},{5,1},{6,4},{7,3},{8,10},{9,13},{10,... | collective-permute-start | bytes 2064392 | tf_op jit(solution)/shard_map/ppermute | solution.py:37
  162.7 11.3 %collective-permute-start.29 = (bf16[4,112,768]{2,1,0:T(8,128)(2,1)S(1)}, bf16[4,112,768]{2,1,0:T(8,128)(2,1)S(1)}, u32[]{:S(2)}, u32[]{:S(2)}) collective-permute-start(bf16[4,112,768]{2,1,0:T(8,128)(2,1)S(1)} %pad_maximum_fusion.3), channel_id=1, source_target_pairs={{0,2},{1,5},{2,0},{3,7},{4,6},{5,1},{6,4},{7,3},{8,10},{9,13},{10,... | collective-permute-start | bytes 2064392 | tf_op jit(solution)/shard_map/ppermute | solution.py:37
  164.7 22.0 %collective-permute-start.30 = (bf16[4,112,768]{2,1,0:T(8,128)(2,1)S(1)}, bf16[4,112,768]{2,1,0:T(8,128)(2,1)S(1)}, u32[]{:S(2)}, u32[]{:S(2)}) collective-permute-start(bf16[4,112,768]{2,1,0:T(8,128)(2,1)S(1)} %pad_maximum_fusion.6), channel_id=1, source_target_pairs={{0,16},{1,9},{2,18},{3,11},{4,20},{5,13},{6,22},{7,15},{8,24},{9,1... | collective-permute-start | bytes 2064392 | tf_op jit(solution)/shard_map/ppermute | solution.py:37
  174.0 12.7 %collective-permute-start.32 = (bf16[2,2,96,768]{3,2,0,1:T(8,128)(2,1)S(1)}, bf16[2,2,96,768]{3,2,0,1:T(8,128)(2,1)S(1)}, u32[]{:S(2)}, u32[]{:S(2)}) collective-permute-start(bf16[2,2,96,768]{3,2,0,1:T(8,128)(2,1)S(1)} %pad_maximum_fusion.9), channel_id=1, source_target_pairs={{0,4},{1,3},{2,6},{3,1},{4,0},{5,7},{6,2},{7,5},{8,12},{9,11},{10,... | collective-permute-start | bytes 1769480 | tf_op jit(solution)/shard_map/ppermute | solution.py:37
  187.1 6.8 %collective-permute-start.35 = (bf16[1,2,96,768]{3,2,0,1:T(8,128)(2,1)S(1)}, bf16[1,2,96,768]{3,2,0,1:T(8,128)(2,1)S(1)}, u32[]{:S(2)}, u32[]{:S(2)}) collective-permute-start(bf16[1,2,96,768]{3,2,0,1:T(8,128)(2,1)S(1)} %add_convert_fusion.8), channel_id=1, source_target_pairs={{0,8},{1,17},{2,10},{3,19},{4,12},{5,21},{6,14},{7,23},{8,0},{9,25... | collective-permute-start | bytes 884744 | tf_op jit(solution)/shard_map/ppermute | solution.py:37
  187.2 7.6 %collective-permute-start.33 = (bf16[2,112,768]{2,1,0:T(8,128)(2,1)S(1)}, bf16[2,112,768]{2,1,0:T(8,128)(2,1)S(1)}, u32[]{:S(2)}, u32[]{:S(2)}) collective-permute-start(bf16[2,112,768]{2,1,0:T(8,128)(2,1)S(1)} %pad_maximum_fusion.11), channel_id=1, source_target_pairs={{0,4},{1,3},{2,6},{3,1},{4,0},{5,7},{6,2},{7,5},{8,12},{9,11},{10,... | collective-permute-start | bytes 1032200 | tf_op jit(solution)/shard_map/ppermute | solution.py:37
  195.0 5.5 %collective-permute-start.34 = (bf16[1,112,768]{2,1,0:T(8,128)(2,1)S(1)}, bf16[1,112,768]{2,1,0:T(8,128)(2,1)S(1)}, u32[]{:S(2)}, u32[]{:S(2)}) collective-permute-start(bf16[1,112,768]{2,1,0:T(8,128)(2,1)S(1)} %pad_maximum_fusion.15), channel_id=1, source_target_pairs={{0,8},{1,17},{2,10},{3,19},{4,12},{5,21},{6,14},{7,23},{8,0},{9,25... | collective-permute-start | bytes 516104 | tf_op jit(solution)/shard_map/ppermute | solution.py:37
  (8 other events, 34.9 us)

commit v2 on v1

--- a/solution.py
+++ b/solution.py
@@ -547,7 +547,7 @@
         pair.step()
         a.held, pair.held = lax.optimization_barrier((a.held, pair.held))
         b, c = pair.split()
-        a_x = a.step()
+        a_x = a.step(places, slots, turns)
         b_z = b.step()
         a.pieces, b.held = lax.optimization_barrier((a.pieces, b.held))
         attn_w = ready(a.finish())
@@ -670,8 +670,9 @@
         attn_sum.start()
         pair.start()
         attn_sum.end()
+        attn_sum.start()
+        pair.hold(*attn_sum.moved)
         finals = [[part] for part in pair.end()[0]]
-        attn_sum.start()
     else:
         side = jnp.concatenate([side_first, side_second], axis=0)
         finals = []

time: 205 us -> 206 us (level)
  the two profiles are of different devices: /device:TPU:0 before, /device:TPU:16 now
where the time goes in v2:
time: 206 us; the launch traced here: 203 us
  waiting for transfers between devices  80.5 us (39%)
  Pallas kernels  62.6 us (30%)
  starting transfers between devices  39.7 us (19%)
  other arithmetic  9.49 us (5%)
  local copies, waits for them, and re-layouts  8.4 us (4%)
    ppermute x36, waiting for transfers between devices, swap(): return lax.ppermute(array, AXES, list(enumerate(step)))  80.5 us
    pallas_call x10, Pallas kernels, call(): pl.pallas_call(kernel, in_specs=[smem] * len(scalars) + [whole] * len(inp...  62.6 us
    ppermute x36, starting transfers between devices, swap(): return lax.ppermute(array, AXES, list(enumerate(step)))  39.7 us
  transfers between devices with their start and end apart: 36, of which 19 were waited for; matrix products, arithmetic and copies ran while one was open for 6% of the time, Pallas kernels for 28%

profile of v2, /device:TPU:16, one launch (start us, length us, event | category | flops | bytes accessed | tf_op | source)
XLA Modules:
  0.0 202.7 jit_solution(5943669418084303019)
XLA Ops:
  0.7 0.9 copy.39
  1.5 1.0 maximum_bitcast_fusion.1
  2.5 1.6 collective-permute-start
  4.9 0.8 reshape.150
  5.8 1.0 maximum_bitcast_fusion
  6.8 1.4 collective-permute-done
  8.2 2.6 %collective-permute-start.2 = (bf16[1,2,96,768]{3,2,0,1:T(8,128)(2,1)S(1)}, bf16[1,2,96,768]{3,2,0,1:T(8,128)(2,1)S(1)}, u32[]{:S(2)}, u32[]{:S(2)}) collective-permute-start(bf16[1,2,96,768]{3,2,0,1:T(8,128)(2,1)S(1)} %maximum_bitcast_fusion), channel_id=1, source_target_pairs={{0,8},{1,17},{2,10},{3,19},{4,12},{5,21},{6,14},{7,23},{8,0},{9,25... | collective-permute-start | bytes 884744 | tf_op jit(solution)/shard_map/ppermute | solution.py:37
  11.6 1.6 collective-permute-start.1
  13.1 4.9 %collective-permute-done.2 = bf16[1,2,96,768]{3,2,0,1:T(8,128)(2,1)S(1)} collective-permute-done((bf16[1,2,96,768]{3,2,0,1:T(8,128)(2,1)S(1)}, bf16[1,2,96,768]{3,2,0,1:T(8,128)(2,1)S(1)}, u32[]{:S(2)}, u32[]{:S(2)}) %collective-permute-start.2) | collective-permute-done | bytes 294944 | tf_op jit(solution)/shard_map/ppermute | solution.py:37
  19.1 1.7 collective-permute-start.4
  22.1 11.3 %collective-permute-done.3 = bf16[4,96,768]{2,1,0:T(8,128)(2,1)} collective-permute-done((bf16[4,96,768]{2,1,0:T(8,128)(2,1)S(1)}, bf16[4,96,768]{2,1,0:T(8,128)(2,1)}, u32[]{:S(2)}, u32[]{:S(2)}) %collective-permute-start.3) | collective-permute-done | bytes 589856 | tf_op jit(solution)/shard_map/ppermute | solution.py:37
  33.4 1.2 pad_maximum_fusion.rest_1_
  34.7 1.6 collective-permute-start.5
  36.3 0.9 slice_bitcast_fusion
  37.2 3.2 %collective-permute-start.6 = (bf16[4,96,768]{2,1,0:T(8,128)(2,1)S(1)}, bf16[4,96,768]{2,1,0:T(8,128)(2,1)S(1)}, u32[]{:S(2)}, u32[]{:S(2)}) collective-permute-start(bf16[4,96,768]{2,1,0:T(8,128)(2,1)S(1)} %get-tuple-element.225), channel_id=1, source_target_pairs={{0,16},{1,9},{2,18},{3,11},{4,20},{5,13},{6,22},{7,15},{8,24},{9,1... | collective-permute-start | bytes 1769480 | tf_op jit(solution)/shard_map/ppermute | solution.py:37
  40.3 13.7 %collective-permute-done.6 = bf16[4,96,768]{2,1,0:T(8,128)(2,1)S(1)} collective-permute-done((bf16[4,96,768]{2,1,0:T(8,128)(2,1)S(1)}, bf16[4,96,768]{2,1,0:T(8,128)(2,1)S(1)}, u32[]{:S(2)}, u32[]{:S(2)}) %collective-permute-start.6) | collective-permute-done | bytes 589856 | tf_op jit(solution)/shard_map/ppermute | solution.py:37
  55.3 1.8 collective-permute-start.13
  57.1 3.4 %collective-permute-start.12 = (bf16[4,96,768]{2,1,0:T(8,128)(2,1)}, bf16[4,96,768]{2,1,0:T(8,128)(2,1)S(1)}, u32[]{:S(2)}, u32[]{:S(2)}) collective-permute-start(bf16[4,96,768]{2,1,0:T(8,128)(2,1)} %get-tuple-element.116.rest_0_), channel_id=1, source_target_pairs={{0,16},{1,9},{2,18},{3,11},{4,20},{5,13},{6,22},{7,15},{8,24},{9,1... | collective-permute-start | bytes 1769480 | tf_op jit(solution)/shard_map/ppermute | solution.py:37
  60.4 7.6 %shard_map.332 = (bf16[2,768,768]{2,1,0:T(8,128)(2,1)S(1)}, bf16[2,512,576]{2,1,0:T(8,128)(2,1)S(1)}, bf16[2,192,512]{2,1,0:T(8,128)(2,1)S(1)}, bf16[2,3,512,512...) custom-call(s32[32]{0:T(128)S(1)} %get-tuple-element.240.place_ref, ...), custom_call_target="tpu_custom_call" | custom-call | flops 1024 | bytes 1024 | tf_op jit(solution)/shard_map/pallas_call | solution.py:445
  68.1 8.7 %shard_map.333 = (bf16[2,768,768]{2,1,0:T(8,128)(2,1)S(1)}, bf16[2,512,576]{2,1,0:T(8,128)(2,1)S(1)}, bf16[2,192,512]{2,1,0:T(8,128)(2,1)S(1)}, bf16[2,3,512,512...) custom-call(s32[32]{0:T(128)S(1)} %get-tuple-element.240.place_ref, ...), custom_call_target="tpu_custom_call" | custom-call | flops 1024 | bytes 1024 | tf_op jit(solution)/shard_map/pallas_call | solution.py:445
  77.8 2.9 %collective-permute-done.10.rest_2_ = bf16[8,96,768]{2,1,0:T(8,128)(2,1)S(1)} collective-permute-done((bf16[8,96,768]{2,1,0:T(8,128)(2,1)S(1)}, bf16[8,96,768]{2,1,0:T(8,128)(2,1)S(1)}, u32[]{:S(2)}, u32[]{:S(2)}) %collective-permute-start.10) | collective-permute-done | bytes 1179680 | tf_op jit(solution)/shard_map/ppermute | solution.py:37
  80.7 1.0 collective-permute-done.11.rest_3_
  81.7 6.9 %shard_map.334 = (bf16[2,768,768]{2,1,0:T(8,128)(2,1)S(1)}, bf16[2,512,768]{2,1,0:T(8,128)(2,1)S(1)}, bf16[2,512,768]{2,1,0:T(8,128)(2,1)S(1)}, bf16[2,768,768]{...) custom-call(s32[32]{0:T(128)S(1)} %get-tuple-element.240.place_ref, ...), custom_call_target="tpu_custom_call" | custom-call | flops 1024 | bytes 1024 | tf_op jit(solution)/shard_map/pallas_call | solution.py:445
  89.8 2.7 %shard_map.335 = (bf16[2,768,768]{2,1,0:T(8,128)(2,1)S(1)}, f32[512,768]{1,0:T(8,128)S(1)}) custom-call(s32[32]{0:T(128)S(1)} %get-tuple-element.240.place_ref, bf16[2,512,768]{2,1,0:T(8,128)(2,1)S(1)} %get-tuple-element.110.active_ref, f32[512,768]{1,0:T(8,128)S(1)} %get-tuple-element.111.normal_ref.rest_2_, f32[1,768]{1,0:T(1,128)S(1)} %stack.50.rest_1_.first_gain.rest_4_, ...), custom_call_target="tpu_custom_call" | custom-call | flops 1024 | bytes 1024 | tf_op jit(solution)/shard_map/pallas_call | solution.py:445
  93.2 6.2 %shard_map.336 = (bf16[2,768,768]{2,1,0:T(8,128)(2,1)S(1)}, f32[512,768]{1,0:T(8,128)}, f32[512,768]{1,0:T(8,128)S(1)}, bf16[512,768]{1,0:T(8,128)(2,1)S(1)}, bf...) custom-call(s32[32]{0:T(128)S(1)} %get-tuple-element.240.place_ref, ...), custom_call_target="tpu_custom_call" | custom-call | flops 1024 | bytes 1024 | tf_op jit(solution)/shard_map/pallas_call | solution.py:445
  100.2 2.1 %shard_map.337 = bf16[16,96,768]{2,1,0:T(8,128)(2,1)S(1)} custom-call(s32[32]{0:T(128)S(1)} %get-tuple-element.241.slot_ref, bf16[2,512,768]{2,1,0:T(8,128)(2,1)S(1)} %get-tuple-element.110.active_ref, bf16[768,512]{1,0:T(8,128)(2,1)S(1)} %get-tuple-element.123.turned_ref), custom_call_target="tpu_custom_call" | custom-call | flops 1024 | bytes 1024 | tf_op jit(solution)/shard_map/pallas_call | solution.py:445
  102.5 1.7 collective-permute-done.19
  105.3 5.0 %shard_map.338 = (bf16[16,96,768]{2,1,0:T(8,128)(2,1)S(1)}, f32[8,768]{1,0:T(8,128)S(1)}, f32[512,768]{1,0:T(8,128)S(1)}, bf16[768,512]{1,0:T(8,128)(2,1)S(1)}) custom-call(s32[32]{0:T(128)S(1)} %get-tuple-element.241.slot_ref, bf16[512,768]{1,0:T(8,128)(2,1)S(1)} %get-tuple-element.125.low_grad_ref, bf16[2,512,768]{2,1,0:T(8,128)(2,1)S(1)} %get-tuple-element.115.slope_ref, ...), custom_call_target="tpu_custom_call" | custom-call | flops 1024 | bytes 1024 | tf_op jit(solution)/shard_map/pallas_call | solution.py:445
  110.5 1.1 collective-permute-start.21
  111.7 5.8 %shard_map.339 = (bf16[16,96,768]{2,1,0:T(8,128)(2,1)S(1)}, f32[8,768]{1,0:T(8,128)S(1)}, f32[512,768]{1,0:T(8,128)S(1)}, bf16[512,768]{1,0:T(8,128)(2,1)S(1)}, bf16[768,512]{1,0:T(8,128)(2,1)S(1)}) custom-call(s32[32]{0:T(128)S(1)} %get-tuple-element.241.slot_ref, bf16[512,768]{1,0:T(8,128)(2,1)S(1)} %get-tuple-element.125.low_grad_ref, ...), custom_call_target="tpu_custom_call" | custom-call | flops 1024 | bytes 1024 | tf_op jit(solution)/shard_map/pallas_call | solution.py:445
  117.4 3.7 %collective-permute-done.23 = bf16[8,96,768]{2,1,0:T(8,128)(2,1)S(1)} collective-permute-done((bf16[8,96,768]{2,1,0:T(8,128)(2,1)S(1)}, bf16[8,96,768]{2,1,0:T(8,128)(2,1)S(1)}, u32[]{:S(2)}, u32[]{:S(2)}) %collective-permute-start.23) | collective-permute-done | bytes 1179680 | tf_op jit(solution)/shard_map/ppermute | solution.py:37
  122.7 1.8 collective-permute-start.24
  124.7 16.8 %shard_map.340 = (f32[512,768]{1,0:T(8,128)}, f32[2,8,768]{2,1,0:T(8,128)}, f32[2,8,768]{2,1,0:T(8,128)}, bf16[16,112,768]{2,1,0:T(8,128)(2,1)S(1)}, bf16[16,112,768]{2,1,0:T(8,128)(2,1)S(1)}) custom-call(s32[32]{0:T(128)S(1)} %get-tuple-element.241.slot_ref, bf16[768,512]{1,0:T(8,128)(2,1)S(1)} %get-tuple-element.121.turned_ref, ...), custom_call_target="tpu_custom_call" | custom-call | flops 1024 | bytes 1024 | tf_op jit(solution)/shard_map/pallas_call | solution.py:445
  143.4 1.2 collective-permute-start.31
  145.3 1.5 collective-permute-done.27
  147.7 1.8 collective-permute-start.28
  149.8 9.8 %collective-permute-done.31 = bf16[4,96,768]{2,1,0:T(8,128)(2,1)S(1)} collective-permute-done((bf16[4,96,768]{2,1,0:T(8,128)(2,1)S(1)}, bf16[4,96,768]{2,1,0:T(8,128)(2,1)S(1)}, u32[]{:S(2)}, u32[]{:S(2)}) %collective-permute-start.31) | collective-permute-done | bytes 589856 | tf_op jit(solution)/shard_map/ppermute | solution.py:37
  159.6 1.6 collective-permute-start.29
  161.6 2.2 %collective-permute-start.30 = (bf16[4,112,768]{2,1,0:T(8,128)(2,1)S(1)}, bf16[4,112,768]{2,1,0:T(8,128)(2,1)S(1)}, u32[]{:S(2)}, u32[]{:S(2)}) collective-permute-start(bf16[4,112,768]{2,1,0:T(8,128)(2,1)S(1)} %pad_maximum_fusion.6), channel_id=1, source_target_pairs={{0,16},{1,9},{2,18},{3,11},{4,20},{5,13},{6,22},{7,15},{8,24},{9,1... | collective-permute-start | bytes 2064392 | tf_op jit(solution)/shard_map/ppermute | solution.py:37
  164.0 6.6 %collective-permute-done.29 = bf16[4,112,768]{2,1,0:T(8,128)(2,1)S(1)} collective-permute-done((bf16[4,112,768]{2,1,0:T(8,128)(2,1)S(1)}, bf16[4,112,768]{2,1,0:T(8,128)(2,1)S(1)}, u32[]{:S(2)}, u32[]{:S(2)}) %collective-permute-start.29) | collective-permute-done | bytes 688160 | tf_op jit(solution)/shard_map/ppermute | solution.py:37
  170.5 1.6 collective-permute-start.32
  172.6 6.8 %collective-permute-done.30 = bf16[4,112,768]{2,1,0:T(8,128)(2,1)S(1)} collective-permute-done((bf16[4,112,768]{2,1,0:T(8,128)(2,1)S(1)}, bf16[4,112,768]{2,1,0:T(8,128)(2,1)S(1)}, u32[]{:S(2)}, u32[]{:S(2)}) %collective-permute-start.30) | collective-permute-done | bytes 688160 | tf_op jit(solution)/shard_map/ppermute | solution.py:37
  179.4 1.1 collective-permute-done.32
  180.8 5.4 %collective-permute-start.35 = (bf16[1,2,96,768]{3,2,0,1:T(8,128)(2,1)S(1)}, bf16[1,2,96,768]{3,2,0,1:T(8,128)(2,1)S(1)}, u32[]{:S(2)}, u32[]{:S(2)}) collective-permute-start(bf16[1,2,96,768]{3,2,0,1:T(8,128)(2,1)S(1)} %add_convert_fusion.8), channel_id=1, source_target_pairs={{0,8},{1,17},{2,10},{3,19},{4,12},{5,21},{6,14},{7,23},{8,0},{9,25... | collective-permute-start | bytes 884744 | tf_op jit(solution)/shard_map/ppermute | solution.py:37
  186.4 7.1 %collective-permute-done.33 = bf16[2,112,768]{2,1,0:T(8,128)(2,1)S(1)} collective-permute-done((bf16[2,112,768]{2,1,0:T(8,128)(2,1)S(1)}, bf16[2,112,768]{2,1,0:T(8,128)(2,1)S(1)}, u32[]{:S(2)}, u32[]{:S(2)}) %collective-permute-start.33) | collective-permute-done | bytes 344096 | tf_op jit(solution)/shard_map/ppermute | solution.py:37
  193.9 5.4 %collective-permute-done.34.moved_ref = bf16[1,112,768]{2,1,0:T(8,128)(2,1)S(1)} collective-permute-done((bf16[1,112,768]{2,1,0:T(8,128)(2,1)S(1)}, bf16[1,112,768]{2,1,0:T(8,128)(2,1)S(1)}, u32[]{:S(2)}, u32[]{:S(2)}) %collective-permute-start.34) | collective-permute-done | bytes 172064 | tf_op jit(solution)/shard_map/ppermute | solution.py:37
  199.2 0.8 shard_map.341
  201.4 0.8 slice_bitcast_fusion.2
  (172 shorter events, 18.8 us)
Async XLA Ops:
  2.5 5.7 %collective-permute-start = (bf16[1,96,768]{2,1,0:T(8,128)(2,1)S(1)}, bf16[1,96,768]{2,1,0:T(8,128)(2,1)S(1)}, u32[]{:S(2)}, u32[]{:S(2)}) collective-permute-start(bf16[1,96,768]{2,1,0:T(8,128)(2,1)S(1)} %maximum_bitcast_fusion.1), channel_id=1, source_target_pairs={{0,8},{1,17},{2,10},{3,19},{4,12},{5,21},{6,14},{7,23},{8,0},{9,25... | collective-permute-start | bytes 442376 | tf_op jit(solution)/shard_map/ppermute | solution.py:37
  8.2 9.8 %collective-permute-start.2 = (bf16[1,2,96,768]{3,2,0,1:T(8,128)(2,1)S(1)}, bf16[1,2,96,768]{3,2,0,1:T(8,128)(2,1)S(1)}, u32[]{:S(2)}, u32[]{:S(2)}) collective-permute-start(bf16[1,2,96,768]{3,2,0,1:T(8,128)(2,1)S(1)} %maximum_bitcast_fusion), channel_id=1, source_target_pairs={{0,8},{1,17},{2,10},{3,19},{4,12},{5,21},{6,14},{7,23},{8,0},{9,25... | collective-permute-start | bytes 884744 | tf_op jit(solution)/shard_map/ppermute | solution.py:37
  11.6 6.8 %collective-permute-start.1 = (bf16[2,96,768]{2,1,0:T(8,128)(2,1)S(1)}, bf16[2,96,768]{2,1,0:T(8,128)(2,1)S(1)}, u32[]{:S(2)}, u32[]{:S(2)}) collective-permute-start(bf16[2,96,768]{2,1,0:T(8,128)(2,1)S(1)} %pad_maximum_fusion.13), channel_id=1, source_target_pairs={{0,4},{1,3},{2,6},{3,1},{4,0},{5,7},{6,2},{7,5},{8,12},{9,11},{10,... | collective-permute-start | bytes 884744 | tf_op jit(solution)/shard_map/ppermute | solution.py:37
  18.4 15.0 %collective-permute-start.3 = (bf16[4,96,768]{2,1,0:T(8,128)(2,1)S(1)}, bf16[4,96,768]{2,1,0:T(8,128)(2,1)}, u32[]{:S(2)}, u32[]{:S(2)}) collective-permute-start(bf16[4,96,768]{2,1,0:T(8,128)(2,1)S(1)} %pad_maximum_fusion.7), channel_id=1, source_target_pairs={{0,16},{1,9},{2,18},{3,11},{4,20},{5,13},{6,22},{7,15},{8,24},{9,1... | collective-permute-start | bytes 1769480 | tf_op jit(solution)/shard_map/ppermute | solution.py:37
  19.1 15.5 %collective-permute-start.4 = (bf16[2,2,96,768]{3,2,0,1:T(8,128)(2,1)S(1)}, bf16[2,2,96,768]{3,2,0,1:T(8,128)(2,1)S(1)}, u32[]{:S(2)}, u32[]{:S(2)}) collective-permute-start(bf16[2,2,96,768]{3,2,0,1:T(8,128)(2,1)S(1)} %pad_maximum_fusion.8), channel_id=1, source_target_pairs={{0,4},{1,3},{2,6},{3,1},{4,0},{5,7},{6,2},{7,5},{8,12},{9,11},{10,... | collective-permute-start | bytes 1769480 | tf_op jit(solution)/shard_map/ppermute | solution.py:37
  34.7 19.5 %collective-permute-start.5 = (bf16[8,96,768]{2,1,0:T(8,128)(2,1)S(1)}, bf16[8,96,768]{2,1,0:T(8,128)(2,1)}, u32[]{:S(2)}, u32[]{:S(2)}) collective-permute-start(bf16[8,96,768]{2,1,0:T(8,128)(2,1)S(1)} %pad_maximum_fusion.rest_1_), channel_id=1, source_target_pairs={{0,2},{1,5},{2,0},{3,7},{4,6},{5,1},{6,4},{7,3},{8,10},{9,13},{10,... | collective-permute-start | bytes 3538952 | tf_op jit(solution)/shard_map/ppermute | solution.py:37
  37.1 18.1 %copy-start.14 = (f32[768]{0:T(1024)S(1)}, f32[768]{0:T(1024)}, u32[]{:S(2)}) copy-start(f32[768]{0:T(1024)} %param.30) | copy-start | bytes 9220
  37.1 18.1 %copy-start.15 = (f32[768]{0:T(1024)S(1)}, f32[768]{0:T(1024)}, u32[]{:S(2)}) copy-start(f32[768]{0:T(1024)} %param.31) | copy-start | bytes 9220
  37.2 18.1 %copy-start.16 = (f32[768]{0:T(1024)S(1)}, f32[768]{0:T(1024)}, u32[]{:S(2)}) copy-start(f32[768]{0:T(1024)} %param.29) | copy-start | bytes 9220
  37.2 23.3 %copy-start = (bf16[512,768]{1,0:T(8,128)(2,1)S(1)}, bf16[512,768]{1,0:T(8,128)(2,1)}, u32[]{:S(2)}) copy-start(bf16[512,768]{1,0:T(8,128)(2,1)} %tokens_ref.3) | copy-start | bytes 2359300
  37.2 16.9 %collective-permute-start.6 = (bf16[4,96,768]{2,1,0:T(8,128)(2,1)S(1)}, bf16[4,96,768]{2,1,0:T(8,128)(2,1)S(1)}, u32[]{:S(2)}, u32[]{:S(2)}) collective-permute-start(bf16[4,96,768]{2,1,0:T(8,128)(2,1)S(1)} %get-tuple-element.225), channel_id=1, source_target_pairs={{0,16},{1,9},{2,18},{3,11},{4,20},{5,13},{6,22},{7,15},{8,24},{9,1... | collective-permute-start | bytes 1769480 | tf_op jit(solution)/shard_map/ppermute | solution.py:37
  54.2 13.9 %collective-permute-start.7 = (bf16[8,96,768]{2,1,0:T(8,128)(2,1)S(1)}, bf16[8,96,768]{2,1,0:T(8,128)(2,1)}, u32[]{:S(2)}, u32[]{:S(2)}) collective-permute-start(bf16[8,96,768]{2,1,0:T(8,128)(2,1)S(1)} %pad_maximum_fusion.rest_1_), channel_id=1, source_target_pairs={{0,1},{1,0},{2,3},{3,2},{4,5},{5,4},{6,7},{7,6},{8,9},{9,8},{10,11... | collective-permute-start | bytes 3538952 | tf_op jit(solution)/shard_map/ppermute | solution.py:37
  54.2 13.9 %collective-permute-start.8 = (bf16[8,96,768]{2,1,0:T(8,128)(2,1)}, bf16[8,96,768]{2,1,0:T(8,128)(2,1)}, u32[]{:S(2)}, u32[]{:S(2)}) collective-permute-start(bf16[8,96,768]{2,1,0:T(8,128)(2,1)} %collective-permute-done.5.rest_2_), channel_id=1, source_target_pairs={{0,1},{1,0},{2,3},{3,2},{4,5},{5,4},{6,7},{7,6},{8,9},{9,8},{10,11... | collective-permute-start | bytes 3538952 | tf_op jit(solution)/shard_map/ppermute | solution.py:37
  54.7 22.1 %collective-permute-start.9 = (bf16[8,96,768]{2,1,0:T(8,128)(2,1)S(1)}, bf16[8,96,768]{2,1,0:T(8,128)(2,1)}, u32[]{:S(2)}, u32[]{:S(2)}) collective-permute-start(bf16[8,96,768]{2,1,0:T(8,128)(2,1)S(1)} %pad_maximum_fusion.2.rest_0_), channel_id=1, source_target_pairs={{0,2},{1,5},{2,0},{3,7},{4,6},{5,1},{6,4},{7,3},{8,10},{9,13},{10,... | collective-permute-start | bytes 3538952 | tf_op jit(solution)/shard_map/ppermute | solution.py:37
  55.3 22.2 %collective-permute-start.13 = (bf16[4,96,768]{2,1,0:T(8,128)(2,1)}, bf16[4,96,768]{2,1,0:T(8,128)(2,1)S(1)}, u32[]{:S(2)}, u32[]{:S(2)}) collective-permute-start(bf16[4,96,768]{2,1,0:T(8,128)(2,1)} %get-tuple-element.116.rest_0_), channel_id=1, source_target_pairs={{0,2},{1,5},{2,0},{3,7},{4,6},{5,1},{6,4},{7,3},{8,10},{9,13},{10,... | collective-permute-start | bytes 1769480 | tf_op jit(solution)/shard_map/ppermute | solution.py:37
  57.1 20.4 %collective-permute-start.12 = (bf16[4,96,768]{2,1,0:T(8,128)(2,1)}, bf16[4,96,768]{2,1,0:T(8,128)(2,1)S(1)}, u32[]{:S(2)}, u32[]{:S(2)}) collective-permute-start(bf16[4,96,768]{2,1,0:T(8,128)(2,1)} %get-tuple-element.116.rest_0_), channel_id=1, source_target_pairs={{0,16},{1,9},{2,18},{3,11},{4,20},{5,13},{6,22},{7,15},{8,24},{9,1... | collective-permute-start | bytes 1769480 | tf_op jit(solution)/shard_map/ppermute | solution.py:37
  68.1 8.7 %copy-start.2 = (bf16[2,512,576]{2,1,0:T(8,128)(2,1)}, bf16[2,512,576]{2,1,0:T(8,128)(2,1)S(1)}, u32[]{:S(2)}) copy-start(bf16[2,512,576]{2,1,0:T(8,128)(2,1)S(1)} %get-tuple-element.149.rest_7_) | copy-start | bytes 3538948
  68.1 8.7 %copy-start.7 = (bf16[2,192,512]{2,1,0:T(8,128)(2,1)}, bf16[2,192,512]{2,1,0:T(8,128)(2,1)S(1)}, u32[]{:S(2)}) copy-start(bf16[2,192,512]{2,1,0:T(8,128)(2,1)S(1)} %get-tuple-element.150.rest_8_) | copy-start | bytes 1179652
  68.1 13.6 %copy-start.13 = (f32[3072]{0:T(1024)S(1)}, f32[3072]{0:T(1024)}, u32[]{:S(2)}) copy-start(f32[3072]{0:T(1024)} %param.33) | copy-start | bytes 36868
  76.8 11.8 %copy-start.4 = (bf16[2,512,576]{2,1,0:T(8,128)(2,1)}, bf16[2,512,576]{2,1,0:T(8,128)(2,1)S(1)}, u32[]{:S(2)}) copy-start(bf16[2,512,576]{2,1,0:T(8,128)(2,1)S(1)} %get-tuple-element.144.rest_1_) | copy-start | bytes 3538948
  76.8 11.8 %copy-start.9 = (bf16[2,192,512]{2,1,0:T(8,128)(2,1)}, bf16[2,192,512]{2,1,0:T(8,128)(2,1)S(1)}, u32[]{:S(2)}) copy-start(bf16[2,192,512]{2,1,0:T(8,128)(2,1)S(1)} %get-tuple-element.145.rest_2_) | copy-start | bytes 1179652
  76.8 11.8 %copy-start.11 = (f32[512,1]{1,0:T(8,128)}, f32[512,1]{1,0:T(8,128)S(1)}, u32[]{:S(2)}) copy-start(f32[512,1]{1,0:T(8,128)S(1)} %get-tuple-element.106.rest_3_) | copy-start | bytes 6148
  76.9 3.8 %collective-permute-start.10 = (bf16[8,96,768]{2,1,0:T(8,128)(2,1)S(1)}, bf16[8,96,768]{2,1,0:T(8,128)(2,1)S(1)}, u32[]{:S(2)}, u32[]{:S(2)}) collective-permute-start(bf16[8,96,768]{2,1,0:T(8,128)(2,1)S(1)} %pad_maximum_fusion.2.rest_0_), channel_id=1, source_target_pairs={{0,1},{1,0},{2,3},{3,2},{4,5},{5,4},{6,7},{7,6},{8,9},{9,8},{10,11... | collective-permute-start | bytes 3538952 | tf_op jit(solution)/shard_map/ppermute | solution.py:37
  77.0 4.7 %collective-permute-start.11 = (bf16[8,96,768]{2,1,0:T(8,128)(2,1)}, bf16[8,96,768]{2,1,0:T(8,128)(2,1)S(1)}, u32[]{:S(2)}, u32[]{:S(2)}) collective-permute-start(bf16[8,96,768]{2,1,0:T(8,128)(2,1)} %collective-permute-done.9.rest_1_), channel_id=1, source_target_pairs={{0,1},{1,0},{2,3},{3,2},{4,5},{5,4},{6,7},{7,6},{8,9},{9,8},{10,11... | collective-permute-start | bytes 3538952 | tf_op jit(solution)/shard_map/ppermute | solution.py:37
  77.5 11.2 %collective-permute-start.14 = (bf16[4,96,768]{2,1,0:T(8,128)(2,1)S(1)}, bf16[4,96,768]{2,1,0:T(8,128)(2,1)S(1)}, u32[]{:S(2)}, u32[]{:S(2)}) collective-permute-start(bf16[4,96,768]{2,1,0:T(8,128)(2,1)S(1)} %collective-permute-done.12.rest_1_), channel_id=1, source_target_pairs={{0,2},{1,5},{2,0},{3,7},{4,6},{5,1},{6,4},{7,3},{8,10},{9,13},{10,... | collective-permute-start | bytes 1769480 | tf_op jit(solution)/shard_map/ppermute | solution.py:37
  81.7 8.0 %copy-start.18 = (f32[768]{0:T(1024)S(1)}, f32[768]{0:T(1024)}, u32[]{:S(2)}) copy-start(f32[768]{0:T(1024)} %param.36) | copy-start | bytes 9220
  81.7 8.0 %copy-start.19 = (f32[768]{0:T(1024)S(1)}, f32[768]{0:T(1024)}, u32[]{:S(2)}) copy-start(f32[768]{0:T(1024)} %param.37) | copy-start | bytes 9220
  88.6 3.9 %collective-permute-start.15 = (bf16[4,96,768]{2,1,0:T(8,128)(2,1)S(1)}, bf16[4,96,768]{2,1,0:T(8,128)(2,1)S(1)}, u32[]{:S(2)}, u32[]{:S(2)}) collective-permute-start(bf16[4,96,768]{2,1,0:T(8,128)(2,1)S(1)} %copy-done.1), channel_id=1, source_target_pairs={{0,1},{1,0},{2,3},{3,2},{4,5},{5,4},{6,7},{7,6},{8,9},{9,8},{10,11... | collective-permute-start | bytes 1769480 | tf_op jit(solution)/shard_map/ppermute | solution.py:37
  88.8 3.7 %collective-permute-start.16 = (bf16[4,96,768]{2,1,0:T(8,128)(2,1)S(1)}, bf16[4,96,768]{2,1,0:T(8,128)(2,1)S(1)}, u32[]{:S(2)}, u32[]{:S(2)}) collective-permute-start(bf16[4,96,768]{2,1,0:T(8,128)(2,1)S(1)} %collective-permute-done.12.rest_1_), channel_id=1, source_target_pairs={{0,1},{1,0},{2,3},{3,2},{4,5},{5,4},{6,7},{7,6},{8,9},{9,8},{10,11... | collective-permute-start | bytes 1769480 | tf_op jit(solution)/shard_map/ppermute | solution.py:37
  89.2 3.3 %collective-permute-start.17 = (bf16[4,96,768]{2,1,0:T(8,128)(2,1)S(1)}, bf16[4,96,768]{2,1,0:T(8,128)(2,1)S(1)}, u32[]{:S(2)}, u32[]{:S(2)}) collective-permute-start(bf16[4,96,768]{2,1,0:T(8,128)(2,1)S(1)} %collective-permute-done.13.rest_2_), channel_id=1, source_target_pairs={{0,1},{1,0},{2,3},{3,2},{4,5},{5,4},{6,7},{7,6},{8,9},{9,8},{10,11... | collective-permute-start | bytes 1769480 | tf_op jit(solution)/shard_map/ppermute | solution.py:37
  89.3 3.9 %collective-permute-start.18 = (bf16[4,96,768]{2,1,0:T(8,128)(2,1)S(1)}, bf16[4,96,768]{2,1,0:T(8,128)(2,1)S(1)}, u32[]{:S(2)}, u32[]{:S(2)}) collective-permute-start(bf16[4,96,768]{2,1,0:T(8,128)(2,1)S(1)} %collective-permute-done.14.rest_3_), channel_id=1, source_target_pairs={{0,1},{1,0},{2,3},{3,2},{4,5},{5,4},{6,7},{7,6},{8,9},{9,8},{10,11... | collective-permute-start | bytes 1769480 | tf_op jit(solution)/shard_map/ppermute | solution.py:37
  99.6 2.9 %collective-permute-start.22 = (bf16[8,96,768]{2,1,0:T(8,128)(2,1)S(1)}, bf16[8,96,768]{2,1,0:T(8,128)(2,1)S(1)}, u32[]{:S(2)}, u32[]{:S(2)}) collective-permute-start(bf16[8,96,768]{2,1,0:T(8,128)(2,1)S(1)} %get-tuple-element.212), channel_id=1, source_target_pairs={{0,1},{1,0},{2,3},{3,2},{4,5},{5,4},{6,7},{7,6},{8,9},{9,8},{10,11... | collective-permute-start | bytes 3538952 | tf_op jit(solution)/shard_map/ppermute | solution.py:37
  99.8 4.4 %collective-permute-start.19 = (bf16[8,96,768]{2,1,0:T(8,128)(2,1)S(1)}, bf16[8,96,768]{2,1,0:T(8,128)(2,1)S(1)}, u32[]{:S(2)}, u32[]{:S(2)}) collective-permute-start(bf16[8,96,768]{2,1,0:T(8,128)(2,1)S(1)} %get-tuple-element.213), channel_id=1, source_target_pairs={{0,1},{1,0},{2,3},{3,2},{4,5},{5,4},{6,7},{7,6},{8,9},{9,8},{10,11... | collective-permute-start | bytes 3538952 | tf_op jit(solution)/shard_map/ppermute | solution.py:37
  104.9 16.3 %collective-permute-start.23 = (bf16[8,96,768]{2,1,0:T(8,128)(2,1)S(1)}, bf16[8,96,768]{2,1,0:T(8,128)(2,1)S(1)}, u32[]{:S(2)}, u32[]{:S(2)}) collective-permute-start(bf16[8,96,768]{2,1,0:T(8,128)(2,1)S(1)} %get-tuple-element.211), channel_id=1, source_target_pairs={{0,2},{1,5},{2,0},{3,7},{4,6},{5,1},{6,4},{7,3},{8,10},{9,13},{10,... | collective-permute-start | bytes 3538952 | tf_op jit(solution)/shard_map/ppermute | solution.py:37
  110.5 11.0 %collective-permute-start.21 = (bf16[8,96,768]{2,1,0:T(8,128)(2,1)S(1)}, bf16[8,96,768]{2,1,0:T(8,128)(2,1)S(1)}, u32[]{:S(2)}, u32[]{:S(2)}) collective-permute-start(bf16[8,96,768]{2,1,0:T(8,128)(2,1)S(1)} %get-tuple-element.214), channel_id=1, source_target_pairs={{0,1},{1,0},{2,3},{3,2},{4,5},{5,4},{6,7},{7,6},{8,9},{9,8},{10,11... | collective-permute-start | bytes 3538952 | tf_op jit(solution)/shard_map/ppermute | solution.py:37
  111.6 9.9 %collective-permute-start.20 = (bf16[8,96,768]{2,1,0:T(8,128)(2,1)S(1)}, bf16[8,96,768]{2,1,0:T(8,128)(2,1)S(1)}, u32[]{:S(2)}, u32[]{:S(2)}) collective-permute-start(bf16[8,96,768]{2,1,0:T(8,128)(2,1)S(1)} %get-tuple-element.215), channel_id=1, source_target_pairs={{0,1},{1,0},{2,3},{3,2},{4,5},{5,4},{6,7},{7,6},{8,9},{9,8},{10,11... | collective-permute-start | bytes 3538952 | tf_op jit(solution)/shard_map/ppermute | solution.py:37
  122.3 19.3 %collective-permute-start.25 = (bf16[8,96,768]{2,1,0:T(8,128)(2,1)S(1)}, bf16[8,96,768]{2,1,0:T(8,128)(2,1)S(1)}, u32[]{:S(2)}, u32[]{:S(2)}) collective-permute-start(bf16[8,96,768]{2,1,0:T(8,128)(2,1)S(1)} %get-tuple-element.209), channel_id=1, source_target_pairs={{0,2},{1,5},{2,0},{3,7},{4,6},{5,1},{6,4},{7,3},{8,10},{9,13},{10,... | collective-permute-start | bytes 3538952 | tf_op jit(solution)/shard_map/ppermute | solution.py:37
  122.7 18.8 %collective-permute-start.24 = (bf16[4,96,768]{2,1,0:T(8,128)(2,1)S(1)}, bf16[4,96,768]{2,1,0:T(8,128)(2,1)S(1)}, u32[]{:S(2)}, u32[]{:S(2)}) collective-permute-start(bf16[4,96,768]{2,1,0:T(8,128)(2,1)S(1)} %get-tuple-element.157), channel_id=1, source_target_pairs={{0,16},{1,9},{2,18},{3,11},{4,20},{5,13},{6,22},{7,15},{8,24},{9,1... | collective-permute-start | bytes 1769480 | tf_op jit(solution)/shard_map/ppermute | solution.py:37
  141.7 3.2 %collective-permute-start.26 = (bf16[8,112,768]{2,1,0:T(8,128)(2,1)S(1)}, bf16[8,112,768]{2,1,0:T(8,128)(2,1)S(1)}, u32[]{:S(2)}, u32[]{:S(2)}) collective-permute-start(bf16[8,112,768]{2,1,0:T(8,128)(2,1)S(1)} %get-tuple-element.202), channel_id=1, source_target_pairs={{0,1},{1,0},{2,3},{3,2},{4,5},{5,4},{6,7},{7,6},{8,9},{9,8},{10,11... | collective-permute-start | bytes 4128776 | tf_op jit(solution)/shard_map/ppermute | solution.py:37
  142.3 4.5 %collective-permute-start.27 = (bf16[8,112,768]{2,1,0:T(8,128)(2,1)S(1)}, bf16[8,112,768]{2,1,0:T(8,128)(2,1)S(1)}, u32[]{:S(2)}, u32[]{:S(2)}) collective-permute-start(bf16[8,112,768]{2,1,0:T(8,128)(2,1)S(1)} %get-tuple-element.203), channel_id=1, source_target_pairs={{0,1},{1,0},{2,3},{3,2},{4,5},{5,4},{6,7},{7,6},{8,9},{9,8},{10,11... | collective-permute-start | bytes 4128776 | tf_op jit(solution)/shard_map/ppermute | solution.py:37
  143.4 16.3 %collective-permute-start.31 = (bf16[4,96,768]{2,1,0:T(8,128)(2,1)S(1)}, bf16[4,96,768]{2,1,0:T(8,128)(2,1)S(1)}, u32[]{:S(2)}, u32[]{:S(2)}) collective-permute-start(bf16[4,96,768]{2,1,0:T(8,128)(2,1)S(1)} %get-tuple-element.206), channel_id=1, source_target_pairs={{0,16},{1,9},{2,18},{3,11},{4,20},{5,13},{6,22},{7,15},{8,24},{9,1... | collective-permute-start | bytes 1769480 | tf_op jit(solution)/shard_map/ppermute | solution.py:37
  147.7 12.0 %collective-permute-start.28 = (bf16[4,112,768]{2,1,0:T(8,128)(2,1)S(1)}, bf16[4,112,768]{2,1,0:T(8,128)(2,1)S(1)}, u32[]{:S(2)}, u32[]{:S(2)}) collective-permute-start(bf16[4,112,768]{2,1,0:T(8,128)(2,1)S(1)} %pad_maximum_fusion.4), channel_id=1, source_target_pairs={{0,2},{1,5},{2,0},{3,7},{4,6},{5,1},{6,4},{7,3},{8,10},{9,13},{10,... | collective-permute-start | bytes 2064392 | tf_op jit(solution)/shard_map/ppermute | solution.py:37
  159.6 10.9 %collective-permute-start.29 = (bf16[4,112,768]{2,1,0:T(8,128)(2,1)S(1)}, bf16[4,112,768]{2,1,0:T(8,128)(2,1)S(1)}, u32[]{:S(2)}, u32[]{:S(2)}) collective-permute-start(bf16[4,112,768]{2,1,0:T(8,128)(2,1)S(1)} %pad_maximum_fusion.3), channel_id=1, source_target_pairs={{0,2},{1,5},{2,0},{3,7},{4,6},{5,1},{6,4},{7,3},{8,10},{9,13},{10,... | collective-permute-start | bytes 2064392 | tf_op jit(solution)/shard_map/ppermute | solution.py:37
  161.6 17.8 %collective-permute-start.30 = (bf16[4,112,768]{2,1,0:T(8,128)(2,1)S(1)}, bf16[4,112,768]{2,1,0:T(8,128)(2,1)S(1)}, u32[]{:S(2)}, u32[]{:S(2)}) collective-permute-start(bf16[4,112,768]{2,1,0:T(8,128)(2,1)S(1)} %pad_maximum_fusion.6), channel_id=1, source_target_pairs={{0,16},{1,9},{2,18},{3,11},{4,20},{5,13},{6,22},{7,15},{8,24},{9,1... | collective-permute-start | bytes 2064392 | tf_op jit(solution)/shard_map/ppermute | solution.py:37
  170.5 9.9 %collective-permute-start.32 = (bf16[2,2,96,768]{3,2,0,1:T(8,128)(2,1)S(1)}, bf16[2,2,96,768]{3,2,0,1:T(8,128)(2,1)S(1)}, u32[]{:S(2)}, u32[]{:S(2)}) collective-permute-start(bf16[2,2,96,768]{3,2,0,1:T(8,128)(2,1)S(1)} %pad_maximum_fusion.9), channel_id=1, source_target_pairs={{0,4},{1,3},{2,6},{3,1},{4,0},{5,7},{6,2},{7,5},{8,12},{9,11},{10,... | collective-permute-start | bytes 1769480 | tf_op jit(solution)/shard_map/ppermute | solution.py:37
  180.8 20.5 %collective-permute-start.35 = (bf16[1,2,96,768]{3,2,0,1:T(8,128)(2,1)S(1)}, bf16[1,2,96,768]{3,2,0,1:T(8,128)(2,1)S(1)}, u32[]{:S(2)}, u32[]{:S(2)}) collective-permute-start(bf16[1,2,96,768]{3,2,0,1:T(8,128)(2,1)S(1)} %add_convert_fusion.8), channel_id=1, source_target_pairs={{0,8},{1,17},{2,10},{3,19},{4,12},{5,21},{6,14},{7,23},{8,0},{9,25... | collective-permute-start | bytes 884744 | tf_op jit(solution)/shard_map/ppermute | solution.py:37
  186.2 7.3 %collective-permute-start.33 = (bf16[2,112,768]{2,1,0:T(8,128)(2,1)S(1)}, bf16[2,112,768]{2,1,0:T(8,128)(2,1)S(1)}, u32[]{:S(2)}, u32[]{:S(2)}) collective-permute-start(bf16[2,112,768]{2,1,0:T(8,128)(2,1)S(1)} %pad_maximum_fusion.11), channel_id=1, source_target_pairs={{0,4},{1,3},{2,6},{3,1},{4,0},{5,7},{6,2},{7,5},{8,12},{9,11},{10,... | collective-permute-start | bytes 1032200 | tf_op jit(solution)/shard_map/ppermute | solution.py:37
  193.7 5.5 %collective-permute-start.34 = (bf16[1,112,768]{2,1,0:T(8,128)(2,1)S(1)}, bf16[1,112,768]{2,1,0:T(8,128)(2,1)S(1)}, u32[]{:S(2)}, u32[]{:S(2)}) collective-permute-start(bf16[1,112,768]{2,1,0:T(8,128)(2,1)S(1)} %pad_maximum_fusion.15), channel_id=1, source_target_pairs={{0,8},{1,17},{2,10},{3,19},{4,12},{5,21},{6,14},{7,23},{8,0},{9,25... | collective-permute-start | bytes 516104 | tf_op jit(solution)/shard_map/ppermute | solution.py:37
  (8 other events, 32.3 us)
